TPU v7x, 32 devices: a whole 2x2x4 slice. The times are simulated.
32 devices in a mesh: seq: 16 (over z, y, x), chan: 2 (over core).
Axes of the slice: x: 2, y: 2, z: 4, core: 2. Of those that a mesh axis runs over, the one named last changes fastest.
Arguments:
- gate_outer: bfloat16 [2048, 4096], P('seq', 'chan'), may hold values from -520 to 520
- gate_inner: bfloat16 [2048, 4096], P('seq', 'chan'), may hold values from -6 to 6
- value_in: bfloat16 [2048, 4096], P('seq', 'chan'), may hold values from -6 to 6
- pole_rates: float32 [8, 4096], P(None, 'chan'), may hold values from 0 to 1, as said below
- pole_weights: float32 [8, 4096], P(None, 'chan'), may hold values from -4 to 4
- skip_gain: float32 [4096], P('chan'), may hold values from -1 to 1
- query_rows: bfloat16 [2048, 4096], P('seq', 'chan'), may hold values from -6 to 6
- key_rows: bfloat16 [2048, 4096], P('seq', 'chan'), may hold values from -6 to 6
Outputs:
- mixed: bfloat16 [2048, 4096], P('seq', 'chan')
Inputs may be any that keep to these rules, and one draw needn't show every extreme that they name: `pole_rates`: each rate is positive and at most 1/30.
All inputs are finite; a program needn't handle non-finite values.
Results may differ from a plain program's by a relative error of at most 0.0065.
Values may be sent and summed in bfloat16 or wider, within the bound.
No kernel may reach another device: no remote copies, remote signals or barrier semaphores. Data moves between devices by JAX's collectives and lax.ppermute only.
A program may use at most 128 MiB of HBM per device.

v0:
```python
import math

import jax
import jax.numpy as jnp
from jax import lax
from jax.sharding import PartitionSpec as P

HD = 128


def prefix(part, axis, combine, identity):
    place = lax.axis_index(axis)
    gathered = jax.tree.map(lambda a: lax.all_gather(a, axis), part)
    state = jax.tree.map(lambda a, e: jnp.zeros_like(a) + jnp.asarray(e, a.dtype), part, identity)

    def one(turn, state):
        return combine(
            state, jax.tree.map(lambda a: lax.dynamic_index_in_dim(a, turn, 0, False), gathered)
        )

    return lax.fori_loop(0, place, one, state)


def block_update(carried, queries, query_pos, key_part, value_part, key_start, score_scale):
    run_max, run_sum, run_acc = carried
    heads_here = run_max.shape[0]
    key_count = key_part.shape[0]
    query_heads = queries.reshape(queries.shape[0], heads_here, -1)
    key_heads = key_part.reshape(key_count, heads_here, -1)
    value_heads = value_part.reshape(key_count, heads_here, -1)
    scores = (
        jnp.einsum("qhd,khd->hqk", query_heads, key_heads, preferred_element_type=jnp.float32)
        * score_scale
    )
    key_pos = key_start + jnp.arange(key_count, dtype=jnp.int32)
    visible = key_pos[None, None, :] <= query_pos[None, :, None]
    scores = jnp.where(visible, scores, -1e30)
    new_max = jnp.maximum(run_max, jnp.max(scores, axis=2))
    rescale = jnp.exp(run_max - new_max)
    expo = jnp.where(visible, jnp.exp(scores - new_max[:, :, None]), 0.0)
    new_sum = run_sum * rescale + jnp.sum(expo, axis=2)
    new_acc = run_acc * rescale[:, :, None] + jnp.einsum(
        "hqk,khd->hqd", expo.astype(jnp.bfloat16), value_heads, preferred_element_type=jnp.float32
    )
    return (new_max, new_sum, new_acc)


def fold_keys(carried, queries, query_pos, pieces, score_scale):
    key_piece, value_piece = pieces
    count_rows = key_piece.shape[0]
    step_rows = math.gcd(count_rows, 1024)

    def one_step(step_index, current):
        sub_start = step_index * step_rows
        key_part = lax.dynamic_slice_in_dim(key_piece, sub_start, step_rows, 0)
        value_part = lax.dynamic_slice_in_dim(value_piece, sub_start, step_rows, 0)
        return block_update(
            current, queries, query_pos, key_part, value_part, sub_start, score_scale
        )

    return lax.fori_loop(0, count_rows // step_rows, one_step, carried)


def finish(carried):
    run_max, run_sum, run_acc = carried
    normed = run_acc / run_sum[:, :, None]
    heads_here, rows_here, depth = normed.shape
    return (
        jnp.transpose(normed, (1, 0, 2)).reshape(rows_here, heads_here * depth).astype(jnp.bfloat16)
    )


def local(
    gate_outer, gate_inner, value_in, pole_rates, pole_weights, skip_gain, query_rows, key_rows
):
    tok_rows, width = gate_outer.shape
    poles_here = pole_rates.shape[0]
    seq_index = lax.axis_index("seq")
    chan_count = lax.axis_size("chan")
    gated = gate_inner.astype(jnp.float32) * value_in.astype(jnp.float32)
    offsets = jnp.arange(tok_rows, dtype=jnp.float32)
    growth = jnp.exp(offsets[:, None, None] * pole_rates[None, :, :])
    weighted = growth * gated[:, None, :]
    lower = (jnp.arange(tok_rows)[:, None] >= jnp.arange(tok_rows)[None, :]).astype(jnp.float32)
    running = jnp.dot(
        lower, weighted.reshape(tok_rows, poles_here * width), precision=lax.Precision.HIGHEST
    )
    running = running.reshape(tok_rows, poles_here, width)
    block_span = jnp.float32(tok_rows)
    summary = running[-1] * jnp.exp(-(block_span - 1.0) * pole_rates)

    def chain_states(earlier, later):
        fade = jnp.exp(-block_span * later[1] * pole_rates)
        return (later[0] + fade * earlier[0], earlier[1] + later[1])

    identity = (jnp.zeros_like(summary), jnp.zeros((1, 1), jnp.float32))
    carry_in, block_count = prefix(
        (summary, jnp.ones((1, 1), jnp.float32)), "seq", chain_states, identity
    )
    decayed = jnp.exp(-offsets[:, None, None] * pole_rates[None, :, :])
    modal = decayed * (running + (jnp.exp(-pole_rates) * carry_in)[None, :, :])
    filtered = jnp.sum(modal * (pole_weights * jnp.sqrt(pole_rates))[None, :, :], axis=1)
    conv_out = gate_outer.astype(jnp.float32) * (filtered + skip_gain[None, :] * gated)
    local_squares = jnp.sum(conv_out * conv_out, axis=1)
    total_squares = lax.psum(local_squares, "chan")
    mean_square = total_squares / (width * chan_count)
    values = (conv_out * lax.rsqrt(mean_square[:, None] + 1e-06)).astype(jnp.bfloat16)
    score_scale = HD ** (-0.5)
    heads_here = width // HD
    my_start = seq_index * tok_rows
    all_pos = my_start + jnp.arange(tok_rows, dtype=jnp.int32)
    final_state = fold_keys(
        (
            jnp.full((heads_here, tok_rows), -1e30, jnp.float32),
            jnp.zeros((heads_here, tok_rows), jnp.float32),
            jnp.zeros((heads_here, tok_rows, HD), jnp.float32),
        ),
        query_rows,
        all_pos,
        (
            lax.all_gather(key_rows, "seq", axis=0, tiled=True),
            lax.all_gather(values, "seq", axis=0, tiled=True),
        ),
        score_scale,
    )
    mixed = finish(final_state)
    return mixed


def solution(mesh):
    in_specs = (
        P("seq", "chan"),
        P("seq", "chan"),
        P("seq", "chan"),
        P(None, "chan"),
        P(None, "chan"),
        P("chan"),
        P("seq", "chan"),
        P("seq", "chan"),
    )
    out_specs = P("seq", "chan")
    return jax.shard_map(local, mesh=mesh, in_specs=in_specs, out_specs=out_specs, check_vma=False)
```

profile of v0, /device:TPU:0, one launch (start us, length us, event | category | flops | bytes accessed | tf_op | source)
XLA Modules:
  0.0 393.7 jit_solution(4399943131139686331)
XLA Ops:
  6.5 0.9 copy.35
  7.4 1.3 convert_multiply_fusion
  8.7 1.0 mul.170
  9.8 7.1 %copy.36 = f32[16,8,8,2048]{3,1,2,0:T(8,128)S(1)} copy(f32[16,8,8,2048]{3,2,1,0:T(8,128)S(1)} %bitcast.77) | data formatting | bytes 16777216
  16.9 6.1 %fusion.25 = f32[128,16384]{1,0:T(8,128)S(1)} fusion(f32[128,16384]{1,0:T(8,128)S(1)} %bitcast.76, f32[16384]{0:T(1024)S(1)} %bitcast.79), kind=kOutput, calls=%fused_computation.35 | convolution fusion | flops 3225436160 | bytes 16842752 | tf_op jit(solution)/shard_map/dot_general | solution.py:85
  23.1 3.2 copy-done.1
  26.5 0.6 exponential_multiply_fusion
  27.2 1.0 copy.26
  28.3 13.8 %copy.37 = f32[16,8,8,2048]{3,2,1,0:T(8,128)} copy(f32[16,8,8,2048]{3,1,2,0:T(8,128)} %bitcast.75) | data formatting | bytes 16777216
  42.1 0.6 dynamic-slice
  42.7 0.7 dynamic-update-slice
  43.5 43.6 %all-reduce = f32[16]{0:T(128)S(1)} all-reduce(f32[16]{0:T(128)S(1)} %dynamic-update-slice), channel_id=1, replica_groups=mesh['seq'=16,'chan'=2] {'seq'}, use_global_device_ids=true, to_apply=%add | all-reduce | flops 16 | bytes 128
  87.2 6.1 %fusion.24 = f32[128,2048]{1,0:T(8,128)S(1)} fusion(f32[16,8,8,2048]{3,2,1,0:T(8,128)} %copy.37, f32[8,2048]{1,0:T(8,128)S(1)} %get-tuple-element.270, f32[8,2048]{1,0:T(8,128)S(1)} %get-tuple-element.269, f32[8,2048]{1,0:T(8,128)S(1)} %get-tuple-element.434, f32[128]{0:T(128)S(1)} %iota_negate_fusion), kind=kLoop, calls=%fused_computation.34 | loop fusion | flops 10223616 | bytes 9634304 | tf_op jit(solution)/shard_map/reduce_sum | solution.py:102
  93.3 1.4 multiply_reduce_fusion
  94.7 2.7 psum.7
  97.4 2.2 multiply_convert_fusion
  99.7 129.8 %all-gather.5.cloned.1.call-done = bf16[2048,2048]{0,1:T(8,128)(2,1)} async-done(((bf16[128,2048]{0,1:T(8,128)(2,1)}), bf16[2048,2048]{0,1:T(8,128)(2,1)}) %all-gather.5.cloned.1.call-update) | async-done | bytes 8388624 | tf_op jit(solution)/shard_map/all_gather | solution.py:121
  229.4 113.8 %all-gather.7.cloned.1.call-done = bf16[2048,2048]{1,0:T(8,128)(2,1)} async-done(((bf16[128,2048]{1,0:T(8,128)(2,1)}), bf16[2048,2048]{1,0:T(8,128)(2,1)}) %all-gather.7.cloned.1.call-update) | async-done | bytes 8388624 | tf_op jit(solution)/shard_map/all_gather | solution.py:122
  343.3 42.7 %while.31 = (s32[]{:T(128)}, f32[16,128]{1,0:T(8,128)S(1)}, f32[16,128]{1,0:T(8,128)S(1)}, f32[16,128,128]{2,1,0:T(8,128)S(1)}, bf16[2048,2048]{0,1:T(8,128)(2,1...) while((s32[]{:T(128)}, f32[16,128]{1,0:T(8,128)S(1)}, ...), condition=%wide.region_8.9_spmd.clone, body=%wide.region_5.8_spmd.clone.sunk | while | flops 1101933696 | bytes 78783712 | solution.py:61
  343.5 4.7 %constant_dynamic-slice_fusion.6 = bf16[1024,2048]{1,0:T(8,128)(2,1)} fusion(bf16[2048,2048]{1,0:T(8,128)(2,1)} %get-tuple-element.423, s32[]{:T(128)S(6)} %select_n.66), kind=kLoop, calls=%fused_computation.26.clone.1 | loop fusion | bytes 8388612 | tf_op jit(solution)/shard_map/while/body/eval_jaxpr/dynamic_slice | solution.py:56
  348.2 6.4 %copy.48 = bf16[1024,2048]{0,1:T(8,128)(2,1)} copy(bf16[1024,2048]{1,0:T(8,128)(2,1)} %constant_dynamic-slice_fusion.6) | data formatting | bytes 8388608 | tf_op jit(solution)/shard_map/while/body/eval_jaxpr/dynamic_slice | solution.py:56
  354.6 2.6 constant_dynamic-slice_fusion.5
  357.3 2.1 fusion.51
  359.4 2.0 fusion.52
  361.4 3.2 fusion.54
  364.9 4.7 %constant_dynamic-slice_fusion.6 = bf16[1024,2048]{1,0:T(8,128)(2,1)} fusion(bf16[2048,2048]{1,0:T(8,128)(2,1)} %get-tuple-element.423, s32[]{:T(128)S(6)} %select_n.66), kind=kLoop, calls=%fused_computation.26.clone.1 | loop fusion | bytes 8388612 | tf_op jit(solution)/shard_map/while/body/eval_jaxpr/dynamic_slice | solution.py:56
  369.6 6.4 %copy.48 = bf16[1024,2048]{0,1:T(8,128)(2,1)} copy(bf16[1024,2048]{1,0:T(8,128)(2,1)} %constant_dynamic-slice_fusion.6) | data formatting | bytes 8388608 | tf_op jit(solution)/shard_map/while/body/eval_jaxpr/dynamic_slice | solution.py:56
  376.0 2.6 constant_dynamic-slice_fusion.5
  378.7 2.1 fusion.51
  380.8 2.0 fusion.52
  382.8 3.2 fusion.54
  386.0 1.1 copy_bitcast_fusion
  (51 shorter events, 0.9 us)
Async XLA Ops:
  6.5 80.5 %all-gather.9.cloned.1.call-start = ((), (), s32[]{:S(2)}) async-start(), calls=%async_computation.2 | async-start | bytes 1114112 | tf_op jit(solution)/shard_map/all_gather | solution.py:13
  16.9 9.6 %copy-start.3 = (f32[8,2048]{1,0:T(8,128)S(1)}, f32[8,2048]{1,0:T(8,128)}, u32[]{:S(2)}) copy-start(f32[8,2048]{1,0:T(8,128)} %param.15) | copy-start | bytes 196612
  16.9 10.3 %copy-start.6 = (bf16[128,2048]{1,0:T(8,128)(2,1)S(1)}, bf16[128,2048]{1,0:T(8,128)(2,1)}, u32[]{:S(2)}) copy-start(bf16[128,2048]{1,0:T(8,128)(2,1)} %param.19) | copy-start | bytes 1572868
  23.1 3.2 copy-start.1
  27.2 202.2 %all-gather.5.cloned.1.call-start = ((), (), s32[]{:S(2)}) async-start(), calls=%async_computation | async-start | bytes 8912896 | tf_op jit(solution)/shard_map/all_gather | solution.py:121
  28.3 315.0 %all-gather.7.cloned.1.call-start = ((), (), s32[]{:S(2)}) async-start(), calls=%async_computation.1 | async-start | bytes 8912896 | tf_op jit(solution)/shard_map/all_gather | solution.py:122
  28.3 13.8 %copy-start.9 = (u32[32]{0:T(128)S(1)}, u32[32]{0:T(128)}, u32[]{:S(2)}) copy-start(u32[32]{0:T(128)} %constant.100) | copy-start | bytes 388
  28.3 58.8 %copy-start.7 = (f32[8,2048]{1,0:T(8,128)S(1)}, f32[8,2048]{1,0:T(8,128)}, u32[]{:S(2)}) copy-start(f32[8,2048]{1,0:T(8,128)} %param.16) | copy-start | bytes 196612
  42.1 51.2 %copy-start.4 = (bf16[128,2048]{1,0:T(8,128)(2,1)S(1)}, bf16[128,2048]{1,0:T(8,128)(2,1)}, u32[]{:S(2)}) copy-start(bf16[128,2048]{1,0:T(8,128)(2,1)} %param.14) | copy-start | bytes 1572868
  42.1 51.2 %copy-start.5 = (bf16[128,2048]{1,0:T(8,128)(2,1)S(1)}, bf16[128,2048]{1,0:T(8,128)(2,1)}, u32[]{:S(2)}) copy-start(bf16[128,2048]{1,0:T(8,128)(2,1)} %param.13) | copy-start | bytes 1572868
  42.1 51.2 %copy-start.8 = (f32[2048]{0:T(1024)S(1)}, f32[2048]{0:T(1024)}, u32[]{:S(2)}) copy-start(f32[2048]{0:T(1024)} %param.17) | copy-start | bytes 24580
  87.1 256.2 %copy-start.2 = (bf16[128,2048]{1,0:T(8,128)(2,1)S(1)}, bf16[128,2048]{1,0:T(8,128)(2,1)}, u32[]{:S(2)}) copy-start(bf16[128,2048]{1,0:T(8,128)(2,1)} %param.18) | copy-start | bytes 1572868
  357.3 4.2 %copy-start = (bf16[1024,2048]{0,1:T(8,128)(2,1)S(1)}, bf16[1024,2048]{0,1:T(8,128)(2,1)}, u32[]{:S(2)}) copy-start(bf16[1024,2048]{0,1:T(8,128)(2,1)} %copy.48) | copy-start | bytes 12582916 | tf_op jit(solution)/shard_map/while
  378.7 4.2 %copy-start = (bf16[1024,2048]{0,1:T(8,128)(2,1)S(1)}, bf16[1024,2048]{0,1:T(8,128)(2,1)}, u32[]{:S(2)}) copy-start(bf16[1024,2048]{0,1:T(8,128)(2,1)} %copy.48) | copy-start | bytes 12582916 | tf_op jit(solution)/shard_map/while
Sparse Core Ops, SparseCore 0:
  27.3 58.1 all-gather.8
  88.2 141.1 all-gather.4
  232.2 111.0 all-gather.6
where the time goes:
time: 395 us; the launch traced here: 394 us
  waiting for transfers between devices  244 us (62%)
  local copies, waits for them, and re-layouts  56.1 us (14%)
  blocking collectives  46.3 us (12%)
  other arithmetic  17.3 us (4%)
  matrix products  16.7 us (4%)
  between operations  13.3 us (3%)
    all_gather x1, waiting for transfers between devices, local(): lax.all_gather(key_rows, 'seq', axis=0, tiled=True)  130 us
    all_gather x1, waiting for transfers between devices, local(): lax.all_gather(values, 'seq', axis=0, tiled=True)  114 us
    unnamed x1, blocking collectives  43.6 us
    unnamed x25, local copies, waits for them, and re-layouts  27.3 us
    dynamic_slice x4, local copies, waits for them, and re-layouts, one_step(): value_part = lax.dynamic_slice_in_dim(value_piece, sub_start, step_rows, 0)  22.3 us
  transfers between devices with their start and end apart: 3, of which 2 were waited for; matrix products, arithmetic and copies ran while one was open for 7% of the time, Pallas kernels for 0%

commit v1 on v0

v1 whole, which is shorter than its diff:
```python
import functools
import math

import jax
import jax.numpy as jnp
from jax import lax
from jax.experimental import pallas as pl
from jax.experimental.pallas import tpu as pltpu
from jax.sharding import PartitionSpec as P

HD = 128
LOG2E = math.log2(math.e)
VMEM_CAP = 16 * 1024 * 1024


def call(body, out_shape, flops, moved, exps=0, **kwargs):
    return pl.pallas_call(
        body,
        out_shape=out_shape,
        compiler_params=pltpu.CompilerParams(vmem_limit_bytes=VMEM_CAP),
        cost_estimate=pl.CostEstimate(flops=flops, bytes_accessed=moved, transcendentals=exps),
        **kwargs,
    )


def split_kernel(pieces, per_piece, *refs):
    *ins, out = refs
    rows = ins[0].shape[0]
    for place in range(pieces):
        cols = slice(place * per_piece, (place + 1) * per_piece)
        for which, ref in enumerate(ins):
            out[place, which * rows : (which + 1) * rows, :] = ref[:, cols]


def split_heads(arrays, pieces):
    rows, width = arrays[0].shape
    per_piece = width // pieces
    return call(
        functools.partial(split_kernel, pieces, per_piece),
        jax.ShapeDtypeStruct((pieces, rows * len(arrays), per_piece), arrays[0].dtype),
        0,
        4 * rows * width * len(arrays),
    )(*arrays)


def spread(ref, source, count, groups, pitch):
    for group in range(groups):
        ref[pl.ds(group, count, stride=pitch), :] = source[:, group * HD : (group + 1) * HD]


def local_kernel(groups, pitch, gate, value, rates, weights, skip, out, summary, gated, decay, gain, direct):
    rows = gate.shape[0]
    poles = rates.shape[0]
    if pitch != groups:
        for ref in (gated, decay, gain, direct):
            ref[...] = jnp.zeros_like(ref)
    spread(decay, jnp.exp(-rates[...]), poles, groups, pitch)
    spread(gain, weights[...] * jnp.sqrt(rates[...]), poles, groups, pitch)
    spread(direct, skip[...], 1, groups, pitch)
    for group in range(groups):
        cols = slice(group * HD, (group + 1) * HD)
        product = gate[:, cols].astype(jnp.float32) * value[:, cols].astype(jnp.float32)
        gated[pl.ds(group, rows, stride=pitch), :] = product

    fades = [decay[m * pitch : (m + 1) * pitch, :] for m in range(poles)]
    gains = [gain[m * pitch : (m + 1) * pitch, :] for m in range(poles)]
    own = direct[...]

    def one(t, states):
        at = pl.ds(pl.multiple_of(t * pitch, pitch), pitch)
        now = gated[at, :]
        states = [fade * state + now for fade, state in zip(fades, states)]
        terms = [own * now] + [g * state for g, state in zip(gains, states)]
        while len(terms) > 1:
            terms = [a + b for a, b in zip(terms[::2], terms[1::2])] + terms[len(terms) // 2 * 2 :]
        out[at, :] = terms[0]
        return states

    zero = jnp.zeros((pitch, HD), jnp.float32)
    states = lax.fori_loop(0, rows, one, [zero] * poles, unroll=4)
    for m in range(poles):
        summary[m * pitch : (m + 1) * pitch, :] = states[m]


def local_conv(gate, value, rates, weights, skip, pitch):
    rows, width = gate.shape
    poles = rates.shape[0]
    f32 = jnp.float32
    return call(
        functools.partial(local_kernel, width // HD, pitch),
        (
            jax.ShapeDtypeStruct((rows * pitch, HD), f32),
            jax.ShapeDtypeStruct((poles * pitch, HD), f32),
        ),
        4 * poles * rows * width,
        8 * rows * width,
        scratch_shapes=[
            pltpu.VMEM((rows * pitch, HD), f32),
            pltpu.VMEM((poles * pitch, HD), f32),
            pltpu.VMEM((poles * pitch, HD), f32),
            pltpu.VMEM((pitch, HD), f32),
        ],
    )(gate, value, rates, weights, skip)


def tail_kernel(groups, pitch, local, carry, rates, weights, gate, out, squares, full, decay, gain):
    rows = gate.shape[0]
    poles = rates.shape[0]
    if pitch != groups:
        for ref in (decay, gain):
            ref[...] = jnp.zeros_like(ref)
    spread(decay, jnp.exp(-rates[...]), poles, groups, pitch)
    spread(gain, weights[...] * jnp.sqrt(rates[...]), poles, groups, pitch)
    parts = [slice(m * pitch, (m + 1) * pitch) for m in range(poles)]
    fades = [decay[part, :] for part in parts]

    def one(t, states):
        at = pl.ds(pl.multiple_of(t * pitch, pitch), pitch)
        states = [fade * state for fade, state in zip(fades, states)]
        terms = [local[at, :]] + states
        while len(terms) > 1:
            terms = [a + b for a, b in zip(terms[::2], terms[1::2])] + terms[len(terms) // 2 * 2 :]
        full[at, :] = terms[0]
        return states

    lax.fori_loop(0, rows, one, [gain[part, :] * carry[part, :] for part in parts], unroll=4)
    total = jnp.zeros((rows, HD), jnp.float32)
    for group in range(groups):
        cols = slice(group * HD, (group + 1) * HD)
        conv = gate[:, cols].astype(jnp.float32) * full[pl.ds(group, rows, stride=pitch), :]
        out[group] = conv
        total = total + conv * conv
    ones = jnp.ones((8, HD), jnp.float32)
    summed = lax.dot_general(
        ones,
        total,
        (((1,), (1,)), ((), ())),
        precision=lax.Precision.HIGHEST,
        preferred_element_type=jnp.float32,
    )
    squares[...] = summed[0:1, :]


def tail_conv(local, carry, rates, weights, gate, pitch):
    rows, width = gate.shape
    poles = rates.shape[0]
    f32 = jnp.float32
    return call(
        functools.partial(tail_kernel, width // HD, pitch),
        (
            jax.ShapeDtypeStruct((width // HD, rows, HD), f32),
            jax.ShapeDtypeStruct((1, rows), f32),
        ),
        3 * poles * rows * width,
        10 * rows * width,
        scratch_shapes=[
            pltpu.VMEM((rows * pitch, HD), f32),
            pltpu.VMEM((poles * pitch, HD), f32),
            pltpu.VMEM((poles * pitch, HD), f32),
        ],
    )(local, carry, rates, weights, gate)


def norm_kernel(channels, conv, squares, out):
    rows = conv.shape[1]
    scale = lax.rsqrt(squares[...] / channels + 1e-06)
    scale = jnp.transpose(jnp.broadcast_to(scale, (HD, rows)))
    per_chunk = out.shape[2] // HD
    for group in range(conv.shape[0]):
        place, inner = divmod(group, per_chunk)
        out[place, :, inner * HD : (inner + 1) * HD] = (conv[group] * scale).astype(out.dtype)


def normalize(conv, squares, channels, pieces):
    groups, rows, _ = conv.shape
    return call(
        functools.partial(norm_kernel, channels),
        jax.ShapeDtypeStruct((pieces, rows, groups // pieces * HD), jnp.bfloat16),
        groups * rows * HD,
        6 * groups * rows * HD,
    )(conv, squares)


def prefix_state(summary, rates, block_rows, axis):
    size = lax.axis_size(axis)
    place = lax.axis_index(axis)
    span = rates * jnp.float32(block_rows)
    total, before = summary, jnp.zeros_like(summary)
    step = 1
    while step < size:
        many = min(4, size // step)
        mine = place // step % many
        inside = place % step
        others = [
            lax.ppermute(total, axis, [(i, i ^ (step * k)) for i in range(size)])
            for k in range(1, many)
        ]
        new_total = jnp.exp(-span * (step * (many - 1 - mine)).astype(jnp.float32)) * total
        for k, other in enumerate(others, 1):
            its = mine ^ k
            gap = ((mine - 1 - its) * step + inside).astype(jnp.float32)
            fade = jnp.exp(-span * jnp.maximum(gap, 0.0))
            before = before + jnp.where(its < mine, fade * other, 0.0)
            fade = jnp.exp(-span * (step * (many - 1 - its)).astype(jnp.float32))
            new_total = new_total + fade * other
        total = new_total
        step *= many
    return before


def score_kernel(block, inputs, weights, totals, scores):
    chunks, twice, _ = inputs.shape
    rows = twice // 2
    per_block = block // rows
    factor = LOG2E * HD ** (-0.5)
    row = lax.broadcasted_iota(jnp.int32, (block, block), 0)
    col = lax.broadcasted_iota(jnp.int32, (block, block), 1)
    visible = col <= row
    for turn in range(chunks // per_block):
        query = inputs[turn * per_block : (turn + 1) * per_block, 0:rows, :].reshape(block, HD)
        top = None
        for part in range(turn + 1):
            key = inputs[part * per_block : (part + 1) * per_block, rows:, :].reshape(block, HD)
            got = lax.dot_general(
                query, key, (((1,), (1,)), ((), ())), preferred_element_type=jnp.float32
            )
            if part == turn:
                got = jnp.where(visible, got, -1e30)
            scores[:, part * block : (part + 1) * block] = got
            for lane in range(0, block, HD):
                one = got[:, lane : lane + HD]
                top = one if top is None else jnp.maximum(top, one)
        top = jnp.max(top, axis=1, keepdims=True) * factor
        summed = jnp.zeros((block, HD), jnp.float32)
        for part in range(turn + 1):
            expo = jnp.exp2(scores[:, part * block : (part + 1) * block] * factor - top)
            for lane in range(0, block, HD):
                summed = summed + expo[:, lane : lane + HD]
            weights[turn * (turn + 1) // 2 + part] = expo.astype(jnp.bfloat16)
        total = jnp.sum(summed, axis=1, keepdims=True)
        totals[turn * block : (turn + 1) * block, :] = jnp.broadcast_to(total, (block, HD))


def mix_kernel(block, weights, totals, values, out):
    chunks, rows, _ = values.shape
    per_block = block // rows
    for turn in range(chunks // per_block):
        mixed = jnp.zeros((block, HD), jnp.float32)
        for part in range(turn + 1):
            value = values[part * per_block : (part + 1) * per_block].reshape(block, HD)
            mixed = mixed + jnp.dot(
                weights[turn * (turn + 1) // 2 + part], value, preferred_element_type=jnp.float32
            )
        mixed = mixed / totals[turn * block : (turn + 1) * block, :]
        out[turn * per_block : (turn + 1) * per_block] = mixed.astype(out.dtype).reshape(
            per_block, rows, HD
        )


def block_of(chunks, rows):
    block = rows
    while block < 256 and chunks * rows % (2 * block) == 0:
        block *= 2
    return block


def head_weights(pair):
    chunks, twice, _ = pair.shape
    length = chunks * twice // 2
    block = block_of(chunks, twice // 2)
    tiles = (length // block) * (length // block + 1) // 2
    return call(
        functools.partial(score_kernel, block),
        (
            jax.ShapeDtypeStruct((tiles, block, block), jnp.bfloat16),
            jax.ShapeDtypeStruct((length, HD), jnp.float32),
        ),
        tiles * block * block * (2 * HD + 8),
        tiles * block * block * 2,
        tiles * block * block,
        scratch_shapes=[pltpu.VMEM((block, length), jnp.float32)],
    )(pair)


def head_mix(weights, totals, values):
    chunks, rows, _ = values.shape
    block = block_of(chunks, rows)
    return call(
        functools.partial(mix_kernel, block),
        jax.ShapeDtypeStruct((chunks, rows, HD), jnp.bfloat16),
        weights.size * 2 * HD,
        weights.size * 2,
    )(weights, totals, values)


def gathered_head(query, key, value, first_row):
    count, step = key.shape[0], math.gcd(key.shape[0], 1024)
    query_pos = first_row + jnp.arange(query.shape[0], dtype=jnp.int32)

    def one(turn, carried):
        top, total, mixed = carried
        keys = lax.dynamic_slice_in_dim(key, turn * step, step, 0)
        values = lax.dynamic_slice_in_dim(value, turn * step, step, 0)
        scores = jnp.dot(query, keys.T, preferred_element_type=jnp.float32) * HD ** (-0.5)
        visible = (turn * step + jnp.arange(step, dtype=jnp.int32))[None, :] <= query_pos[:, None]
        scores = jnp.where(visible, scores, -1e30)
        new_top = jnp.maximum(top, jnp.max(scores, axis=1, keepdims=True))
        rescale = jnp.exp(top - new_top)
        expo = jnp.where(visible, jnp.exp(scores - new_top), 0.0)
        total = total * rescale + jnp.sum(expo, axis=1, keepdims=True)
        part = jnp.dot(expo.astype(jnp.bfloat16), values, preferred_element_type=jnp.float32)
        return new_top, total, mixed * rescale + part

    rows = query.shape[0]
    start = (
        jnp.full((rows, 1), -1e30, jnp.float32),
        jnp.zeros((rows, 1), jnp.float32),
        jnp.zeros((rows, HD), jnp.float32),
    )
    _, total, mixed = lax.fori_loop(0, count // step, one, start)
    return (mixed / total).astype(jnp.bfloat16)


def local(
    gate_outer, gate_inner, value_in, pole_rates, pole_weights, skip_gain, query_rows, key_rows
):
    rows, width = gate_outer.shape
    heads = width // HD
    size = lax.axis_size("seq")
    channels = width * lax.axis_size("chan")
    group_count = size // heads
    groups = None
    if group_count > 1:
        groups = [list(range(g * heads, (g + 1) * heads)) for g in range(group_count)]
    exchange = functools.partial(
        lax.all_to_all, axis_name="seq", split_axis=0, concat_axis=0, axis_index_groups=groups
    )
    pitch = -(-heads // 8) * 8

    pair = exchange(split_heads([query_rows, key_rows], heads))
    part, summary = local_conv(
        gate_inner, value_in, pole_rates, pole_weights, skip_gain[None, :], pitch
    )
    spread_rates = pole_rates.reshape(-1, heads, HD)
    spread_rates = jnp.pad(spread_rates, ((0, 0), (0, pitch - heads), (0, 0))).reshape(-1, HD)
    carry = prefix_state(summary, spread_rates, rows, "seq")
    conv, squares = tail_conv(part, carry, pole_rates, pole_weights, gate_outer, pitch)
    values = exchange(normalize(conv, lax.psum(squares, "chan"), channels, heads))
    if group_count == 1:
        weights, totals = head_weights(pair)
        mixed = head_mix(weights, totals, values)
    else:
        mine = lax.axis_index("seq") // heads
        others = [list(range(h, size, heads)) for h in range(heads)]
        gather = functools.partial(
            lax.all_gather, axis_name="seq", axis_index_groups=others, tiled=True
        )
        span = heads * rows
        mixed = gathered_head(
            pair[:, :rows].reshape(span, HD),
            gather(pair[:, rows:].reshape(span, HD)),
            gather(values.reshape(span, HD)),
            mine * span,
        ).reshape(heads, rows, HD)
    return jnp.transpose(exchange(mixed), (1, 0, 2)).reshape(rows, width)


def solution(mesh):
    rows = P("seq", "chan")
    poles = P(None, "chan")
    return jax.shard_map(
        local,
        mesh=mesh,
        in_specs=(rows, rows, rows, poles, poles, P("chan"), rows, rows),
        out_specs=rows,
        check_vma=False,
    )
```

time: 395 us -> 92.6 us (0.23)
  waiting for transfers between devices: 244 us -> 27.1 us
  local copies, waits for them, and re-layouts: 56.1 us -> 13.6 us
  blocking collectives: 46.3 us -> 20.7 us
  starting transfers between devices: 0.09 us -> 20.9 us
  other arithmetic: 17.3 us -> 0.17 us
  matrix products: 16.7 us -> 0 us
  between operations: 13.3 us -> 0.16 us
  Pallas kernels: 0 us -> 9.37 us
    all_gather x3 -> x0, waiting for transfers between devices: 244 us -> none  [the longest x1 130 us: local(): lax.all_gather(key_rows, 'seq', axis=0, tiled=True)]
    unnamed x1 -> x0, blocking collectives: 43.6 us -> none
    dynamic_slice x6 -> x0, local copies, waits for them, and re-layouts: 27.6 us -> none  [the longest x4 22.3 us: one_step(): value_part = lax.dynamic_slice_in_dim(value_piece, sub_start, step_rows, 0)]
    all_to_all x0 -> x1, blocking collectives: none -> 18.2 us  [local(): return jnp.transpose(exchange(mixed), (1, 0, 2)).reshape(rows, width)]
    dot_general x5 -> x0, matrix products: 16.7 us -> none  [the longest x2 6.31 us: block_update(): jnp.einsum('hqk,khd->hqd', expo.astype(jnp.bfloat16), value_heads, prefer...]
    ppermute x0 -> x6, waiting for transfers between devices: none -> 16.4 us  [prefix_state(): lax.ppermute(total, axis, [(i, i ^ step * k) for i in range(size)])]
    unnamed x25 -> x24, local copies, waits for them, and re-layouts: 27.3 us -> 12.1 us
    all_to_all x0 -> x2, starting transfers between devices: none -> 12.9 us  [the longest x1 8.31 us: local(): pair = exchange(split_heads([query_rows, key_rows], heads))]
  transfers between devices with their start and end apart: 3 -> 8, of which waited for: 2 -> 5; matrix products, arithmetic and copies ran while one was open for 7% -> 0% of each run, Pallas kernels for 0% -> 7%
where the time goes in v1:
time: 92.6 us; the launch traced here: 91.9 us
  waiting for transfers between devices  27.1 us (29%)
  starting transfers between devices  20.9 us (23%)
  blocking collectives  20.7 us (22%)
  local copies, waits for them, and re-layouts  13.6 us (15%)
  Pallas kernels  9.37 us (10%)
    all_to_all x1, blocking collectives, local(): return jnp.transpose(exchange(mixed), (1, 0, 2)).reshape(rows, width)  18.2 us
    ppermute x6, waiting for transfers between devices, prefix_state(): lax.ppermute(total, axis, [(i, i ^ step * k) for i in range(size)])  16.4 us
    unnamed x24, local copies, waits for them, and re-layouts  12.1 us
    all_to_all x1, waiting for transfers between devices, local(): exchange(normalize(conv, lax.psum(squares, 'chan'), channels, heads))  10.6 us
    all_to_all x1, starting transfers between devices, local(): pair = exchange(split_heads([query_rows, key_rows], heads))  8.31 us
    ppermute x6, starting transfers between devices, prefix_state(): lax.ppermute(total, axis, [(i, i ^ step * k) for i in range(size)])  8 us
    all_to_all x1, starting transfers between devices, local(): exchange(normalize(conv, lax.psum(squares, 'chan'), channels, heads))  4.59 us
    pallas_call x1, Pallas kernels, head_weights(): call(functools.partial(score_kernel, block), (jax.ShapeDtypeStruct((tiles...  2.63 us
  transfers between devices with their start and end apart: 8, of which 5 were waited for; matrix products, arithmetic and copies ran while one was open for 0% of the time, Pallas kernels for 7%

profile of v1, /device:TPU:0, one launch (start us, length us, event | category | flops | bytes accessed | tf_op | source)
XLA Modules:
  0.0 91.9 jit_solution(9135166572906469161)
XLA Ops:
  0.0 1.1 %copy-done.7 = bf16[128,2048]{1,0:T(8,128)(2,1)S(1)} copy-done((bf16[128,2048]{1,0:T(8,128)(2,1)S(1)}, bf16[128,2048]{1,0:T(8,128)(2,1)}, u32[]{:S(2)}) %copy-start.7) | copy-done | bytes 524312
  1.1 1.0 %copy-done.8 = bf16[128,2048]{1,0:T(8,128)(2,1)S(1)} copy-done((bf16[128,2048]{1,0:T(8,128)(2,1)S(1)}, bf16[128,2048]{1,0:T(8,128)(2,1)}, u32[]{:S(2)}) %copy-start.8) | copy-done | bytes 524312
  2.1 1.2 %shard_map.82 = bf16[16,256,128]{2,1,0:T(8,128)(2,1)} custom-call(bf16[128,2048]{1,0:T(8,128)(2,1)S(1)} %copy-done.7, bf16[128,2048]{1,0:T(8,128)(2,1)S(1)} %copy-done.8), custom_call_target="tpu_custom_call" | custom-call | bytes 2097152 | tf_op jit(solution)/shard_map/pallas_call | solution.py:38
  3.3 8.3 %all-to-all-start = ((bf16[16,256,128]{2,1,0:T(8,128)(2,1)}), bf16[16,256,128]{2,1,0:T(8,128)(2,1)S(1)}, u32[]{:S(2)}, u32[]{:S(2)}) async-start(bf16[16,256,128]{2,1,0:T(8,128)(2,1)} %shard_map.82), calls=%async_computation | async-start | bytes 2097152 | tf_op jit(solution)/shard_map/all_to_all | solution.py:340
  11.6 0.8 copy-done.2
  12.5 1.0 %copy-done.5 = bf16[128,2048]{1,0:T(8,128)(2,1)S(1)} copy-done((bf16[128,2048]{1,0:T(8,128)(2,1)S(1)}, bf16[128,2048]{1,0:T(8,128)(2,1)}, u32[]{:S(2)}) %copy-start.5) | copy-done | bytes 524312
  13.5 1.0 %copy-done.6 = bf16[128,2048]{1,0:T(8,128)(2,1)S(1)} copy-done((bf16[128,2048]{1,0:T(8,128)(2,1)S(1)}, bf16[128,2048]{1,0:T(8,128)(2,1)}, u32[]{:S(2)}) %copy-start.6) | copy-done | bytes 524312
  14.5 0.8 copy-done.9
  15.4 0.7 copy-done.11
  16.1 2.0 %shard_map.84 = (f32[2048,128]{1,0:T(8,128)S(1)}, f32[128,128]{1,0:T(8,128)S(1)}) custom-call(bf16[128,2048]{1,0:T(8,128)(2,1)S(1)} %copy-done.5, bf16[128,2048]{1,0:T(8,128)(2,1)S(1)} %copy-done.6, f32[8,2048]{1,0:T(8,128)S(1)} %copy-done.2, f32[8,2048]{1,0:T(8,128)S(1)} %copy-done.9, f32[1,2048]{1,0:T(1,128)S(1)} %bitcast.3), custom_call_target="tpu_custom_call" | custom-call | flops 8388608 | bytes 2097152 | tf_op jit(solution)/shard_map/pallas_call | solution.py:89
  18.1 2.9 %collective-permute-start.2 = (f32[128,128]{1,0:T(8,128)S(1)}, f32[128,128]{1,0:T(8,128)S(1)}, u32[]{:S(2)}, u32[]{:S(2)}) collective-permute-start(f32[128,128]{1,0:T(8,128)S(1)} %get-tuple-element.14), channel_id=1, source_target_pairs={{0,6},{2,4},{4,2},{6,0},{8,14},{10,12},{12,10},{14,8},{16,22},{18,... | collective-permute-start | bytes 196616 | tf_op jit(solution)/shard_map/ppermute | solution.py:195
  21.0 0.6 collective-permute-start.1
  21.5 0.1 collective-permute-start
  21.8 5.5 %collective-permute-done.2 = f32[128,128]{1,0:T(8,128)S(1)} collective-permute-done((f32[128,128]{1,0:T(8,128)S(1)}, f32[128,128]{1,0:T(8,128)S(1)}, u32[]{:S(2)}, u32[]{:S(2)}) %collective-permute-start.2) | collective-permute-done | bytes 65568 | tf_op jit(solution)/shard_map/ppermute | solution.py:195
  27.3 2.4 %collective-permute-done = f32[128,128]{1,0:T(8,128)S(1)} collective-permute-done((f32[128,128]{1,0:T(8,128)S(1)}, f32[128,128]{1,0:T(8,128)S(1)}, u32[]{:S(2)}, u32[]{:S(2)}) %collective-permute-start) | collective-permute-done | bytes 65568 | tf_op jit(solution)/shard_map/ppermute | solution.py:195
  29.8 1.0 %collective-permute-start.4 = (f32[128,128]{1,0:T(8,128)S(1)}, f32[128,128]{1,0:T(8,128)S(1)}, u32[]{:S(2)}, u32[]{:S(2)}) collective-permute-start(f32[128,128]{1,0:T(8,128)S(1)} %multiply_add_fusion), channel_id=1, source_target_pairs={{0,16},{2,18},{4,20},{6,22},{8,24},{10,26},{12,28},{14,30},{16,0},... | collective-permute-start | bytes 196616 | tf_op jit(solution)/shard_map/ppermute | solution.py:195
  30.9 3.3 %collective-permute-start.3 = (f32[128,128]{1,0:T(8,128)S(1)}, f32[128,128]{1,0:T(8,128)S(1)}, u32[]{:S(2)}, u32[]{:S(2)}) collective-permute-start(f32[128,128]{1,0:T(8,128)S(1)} %multiply_add_fusion), channel_id=1, source_target_pairs={{0,8},{2,10},{4,12},{6,14},{8,0},{10,2},{12,4},{14,6},{16,24},{18,... | collective-permute-start | bytes 196616 | tf_op jit(solution)/shard_map/ppermute | solution.py:195
  34.4 1.7 %collective-permute-done.5 = f32[128,128]{1,0:T(8,128)S(1)} collective-permute-done((f32[128,128]{1,0:T(8,128)S(1)}, f32[128,128]{1,0:T(8,128)S(1)}, u32[]{:S(2)}, u32[]{:S(2)}) %collective-permute-start.5) | collective-permute-done | bytes 65568 | tf_op jit(solution)/shard_map/ppermute | solution.py:195
  36.0 6.9 %collective-permute-done.4 = f32[128,128]{1,0:T(8,128)S(1)} collective-permute-done((f32[128,128]{1,0:T(8,128)S(1)}, f32[128,128]{1,0:T(8,128)S(1)}, u32[]{:S(2)}, u32[]{:S(2)}) %collective-permute-start.4) | collective-permute-done | bytes 65568 | tf_op jit(solution)/shard_map/ppermute | solution.py:195
  43.0 1.0 %copy-done.4 = bf16[128,2048]{1,0:T(8,128)(2,1)S(1)} copy-done((bf16[128,2048]{1,0:T(8,128)(2,1)S(1)}, bf16[128,2048]{1,0:T(8,128)(2,1)}, u32[]{:S(2)}) %copy-start.4) | copy-done | bytes 524312
  44.0 1.2 %shard_map.85 = (f32[16,128,128]{2,1,0:T(8,128)S(1)}, f32[1,128]{1,0:T(1,128)S(1)}) custom-call(f32[2048,128]{1,0:T(8,128)S(1)} %get-tuple-element.13.local, f32[128,128]{1,0:T(8,128)S(1)} %select_add_fusion.carry, f32[8,2048]{1,0:T(8,128)S(1)} %copy-done.3, f32[8,2048]{1,0:T(8,128)S(1)} %copy-done.10, bf16[128,2048]{1,0:T(8,128)(2,1)S(1)} %copy-done.4), custom_call_target="tpu_custom_call" | custom-call | flops 6291456 | bytes 2621440 | tf_op jit(solution)/shard_map/pallas_call | solution.py:148
  45.3 2.5 %psum.7.squares = f32[1,128]{1,0:T(1,128)S(1)} all-reduce(f32[1,128]{1,0:T(1,128)S(1)} %get-tuple-element.16), channel_id=1, replica_groups=mesh['seq'=16,'chan'=2] {'chan'}, use_global_device_ids=true, to_apply=%region_0.1 | all-reduce | flops 128 | bytes 1024 | tf_op jit(solution)/shard_map/psum | solution.py:348
  47.7 1.0 %shard_map.86 = bf16[16,128,128]{2,1,0:T(8,128)(2,1)} custom-call(f32[16,128,128]{2,1,0:T(8,128)S(1)} %get-tuple-element.15.conv, f32[1,128]{1,0:T(1,128)S(1)} %psum.7.squares), custom_call_target="tpu_custom_call" | custom-call | flops 262144 | bytes 1572864 | tf_op jit(solution)/shard_map/pallas_call | solution.py:176
  48.7 4.6 %all-to-all-start.1 = ((bf16[16,128,128]{2,1,0:T(8,128)(2,1)}), bf16[16,128,128]{2,1,0:T(8,128)(2,1)S(1)}, u32[]{:S(2)}, u32[]{:S(2)}) async-start(bf16[16,128,128]{2,1,0:T(8,128)(2,1)} %shard_map.86), calls=%async_computation.1 | async-start | bytes 1048576 | tf_op jit(solution)/shard_map/all_to_all | solution.py:348
  53.3 2.6 %shard_map.83 = (bf16[36,256,256]{2,1,0:T(8,128)(2,1)S(1)}, f32[2048,128]{1,0:T(8,128)S(1)}) custom-call(bf16[16,256,128]{2,1,0:T(8,128)(2,1)S(1)} %all-to-all-done.inputs), custom_call_target="tpu_custom_call" | custom-call | flops 622854144 | bytes 4718592 | tf_op jit(solution)/shard_map/pallas_call | solution.py:272
  55.9 2.1 %copy-done = bf16[36,256,256]{2,1,0:T(8,128)(2,1)} copy-done((bf16[36,256,256]{2,1,0:T(8,128)(2,1)}, bf16[36,256,256]{2,1,0:T(8,128)(2,1)S(1)}, u32[]{:S(2)}) %copy-start) | copy-done | bytes 4718616
  58.1 10.6 %all-to-all-done.1.values = bf16[16,128,128]{2,1,0:T(8,128)(2,1)S(1)} async-done(((bf16[16,128,128]{2,1,0:T(8,128)(2,1)}), bf16[16,128,128]{2,1,0:T(8,128)(2,1)S(1)}, u32[]{:S(2)}, u32[]{:S(2)}) %all-to-all-start.1) | async-done | bytes 524320 | tf_op jit(solution)/shard_map/all_to_all | solution.py:348
  68.7 2.3 %copy-done.1 = bf16[36,256,256]{2,1,0:T(8,128)(2,1)S(1)} copy-done((bf16[36,256,256]{2,1,0:T(8,128)(2,1)S(1)}, bf16[36,256,256]{2,1,0:T(8,128)(2,1)}, u32[]{:S(2)}) %copy-start.1) | copy-done | bytes 4718616
  71.1 1.4 %shard_map.87 = bf16[16,128,128]{2,1,0:T(8,128)(2,1)S(1)} custom-call(bf16[36,256,256]{2,1,0:T(8,128)(2,1)S(1)} %copy-done.1, f32[2048,128]{1,0:T(8,128)S(1)} %get-tuple-element.12.totals, bf16[16,128,128]{2,1,0:T(8,128)(2,1)S(1)} %all-to-all-done.1.values), custom_call_target="tpu_custom_call" | custom-call | flops 603979776 | bytes 4718592 | tf_op jit(solution)/shard_map/pallas_call | solution.py:288
  72.4 18.2 %all_to_all.15 = bf16[16,128,128]{2,1,0:T(8,128)(2,1)S(1)} all-to-all(bf16[16,128,128]{2,1,0:T(8,128)(2,1)S(1)} %shard_map.87), channel_id=1, replica_groups=mesh['seq'=16,'chan'=2] {'seq'}, dimensions={0} | all-to-all | bytes 1048576 | tf_op jit(solution)/shard_map/all_to_all | solution.py:365
  90.6 0.3 copy.9
  90.9 1.0 %copy.10 = bf16[128,2048]{1,0:T(8,128)(2,1)} copy(bf16[128,2048]{0,1:T(8,128)(2,1)S(1)} %bitcast.5) | data formatting | bytes 1048576 | tf_op jit(solution)/shard_map/reshape | solution.py:365
  (31 shorter events, 0.5 us)
Async XLA Ops:
  0.0 21.6 %copy-start.3 = (f32[8,2048]{1,0:T(8,128)S(1)}, f32[8,2048]{1,0:T(8,128)}, u32[]{:S(2)}) copy-start(f32[8,2048]{1,0:T(8,128)} %rates.3) | copy-start | bytes 196612
  0.0 1.1 %copy-start.7 = (bf16[128,2048]{1,0:T(8,128)(2,1)S(1)}, bf16[128,2048]{1,0:T(8,128)(2,1)}, u32[]{:S(2)}) copy-start(bf16[128,2048]{1,0:T(8,128)(2,1)} %refs_0_.1) | copy-start | bytes 1572868
  1.1 1.0 %copy-start.8 = (bf16[128,2048]{1,0:T(8,128)(2,1)S(1)}, bf16[128,2048]{1,0:T(8,128)(2,1)}, u32[]{:S(2)}) copy-start(bf16[128,2048]{1,0:T(8,128)(2,1)} %refs_1_.1) | copy-start | bytes 1572868
  2.1 40.8 %copy-start.10 = (f32[8,2048]{1,0:T(8,128)S(1)}, f32[8,2048]{1,0:T(8,128)}, u32[]{:S(2)}) copy-start(f32[8,2048]{1,0:T(8,128)} %weights.3) | copy-start | bytes 196612
  3.3 45.4 %all-to-all-start = ((bf16[16,256,128]{2,1,0:T(8,128)(2,1)}), bf16[16,256,128]{2,1,0:T(8,128)(2,1)S(1)}, u32[]{:S(2)}, u32[]{:S(2)}) async-start(bf16[16,256,128]{2,1,0:T(8,128)(2,1)} %shard_map.82), calls=%async_computation | async-start | bytes 2097152 | tf_op jit(solution)/shard_map/all_to_all | solution.py:340
  11.6 0.8 copy-start.2
  12.5 1.0 %copy-start.5 = (bf16[128,2048]{1,0:T(8,128)(2,1)S(1)}, bf16[128,2048]{1,0:T(8,128)(2,1)}, u32[]{:S(2)}) copy-start(bf16[128,2048]{1,0:T(8,128)(2,1)} %gate.2) | copy-start | bytes 1572868
  13.5 1.0 %copy-start.6 = (bf16[128,2048]{1,0:T(8,128)(2,1)S(1)}, bf16[128,2048]{1,0:T(8,128)(2,1)}, u32[]{:S(2)}) copy-start(bf16[128,2048]{1,0:T(8,128)(2,1)} %value.1) | copy-start | bytes 1572868
  14.5 0.8 copy-start.9
  15.4 0.7 copy-start.11
  18.1 9.3 %collective-permute-start.2 = (f32[128,128]{1,0:T(8,128)S(1)}, f32[128,128]{1,0:T(8,128)S(1)}, u32[]{:S(2)}, u32[]{:S(2)}) collective-permute-start(f32[128,128]{1,0:T(8,128)S(1)} %get-tuple-element.14), channel_id=1, source_target_pairs={{0,6},{2,4},{4,2},{6,0},{8,14},{10,12},{12,10},{14,8},{16,22},{18,... | collective-permute-start | bytes 196616 | tf_op jit(solution)/shard_map/ppermute | solution.py:195
  21.0 6.4 %collective-permute-start.1 = (f32[128,128]{1,0:T(8,128)S(1)}, f32[128,128]{1,0:T(8,128)S(1)}, u32[]{:S(2)}, u32[]{:S(2)}) collective-permute-start(f32[128,128]{1,0:T(8,128)S(1)} %get-tuple-element.14), channel_id=1, source_target_pairs={{0,4},{2,6},{4,0},{6,2},{8,12},{10,14},{12,8},{14,10},{16,20},{18,... | collective-permute-start | bytes 196616 | tf_op jit(solution)/shard_map/ppermute | solution.py:195
  21.5 8.2 %collective-permute-start = (f32[128,128]{1,0:T(8,128)S(1)}, f32[128,128]{1,0:T(8,128)S(1)}, u32[]{:S(2)}, u32[]{:S(2)}) collective-permute-start(f32[128,128]{1,0:T(8,128)S(1)} %get-tuple-element.14), channel_id=1, source_target_pairs={{0,2},{2,0},{4,6},{6,4},{8,10},{10,8},{12,14},{14,12},{16,18},{18,... | collective-permute-start | bytes 196616 | tf_op jit(solution)/shard_map/ppermute | solution.py:195
  29.8 6.3 %collective-permute-start.5 = (f32[128,128]{1,0:T(8,128)S(1)}, f32[128,128]{1,0:T(8,128)S(1)}, u32[]{:S(2)}, u32[]{:S(2)}) collective-permute-start(f32[128,128]{1,0:T(8,128)S(1)} %multiply_add_fusion), channel_id=1, source_target_pairs={{0,24},{2,26},{4,28},{6,30},{8,16},{10,18},{12,20},{14,22},{16,8},... | collective-permute-start | bytes 196616 | tf_op jit(solution)/shard_map/ppermute | solution.py:195
  29.8 13.1 %collective-permute-start.4 = (f32[128,128]{1,0:T(8,128)S(1)}, f32[128,128]{1,0:T(8,128)S(1)}, u32[]{:S(2)}, u32[]{:S(2)}) collective-permute-start(f32[128,128]{1,0:T(8,128)S(1)} %multiply_add_fusion), channel_id=1, source_target_pairs={{0,16},{2,18},{4,20},{6,22},{8,24},{10,26},{12,28},{14,30},{16,0},... | collective-permute-start | bytes 196616 | tf_op jit(solution)/shard_map/ppermute | solution.py:195
  30.9 12.0 %collective-permute-start.3 = (f32[128,128]{1,0:T(8,128)S(1)}, f32[128,128]{1,0:T(8,128)S(1)}, u32[]{:S(2)}, u32[]{:S(2)}) collective-permute-start(f32[128,128]{1,0:T(8,128)S(1)} %multiply_add_fusion), channel_id=1, source_target_pairs={{0,8},{2,10},{4,12},{6,14},{8,0},{10,2},{12,4},{14,6},{16,24},{18,... | collective-permute-start | bytes 196616 | tf_op jit(solution)/shard_map/ppermute | solution.py:195
  43.0 1.0 %copy-start.4 = (bf16[128,2048]{1,0:T(8,128)(2,1)S(1)}, bf16[128,2048]{1,0:T(8,128)(2,1)}, u32[]{:S(2)}) copy-start(bf16[128,2048]{1,0:T(8,128)(2,1)} %gate.3) | copy-start | bytes 1572868
  48.7 20.0 %all-to-all-start.1 = ((bf16[16,128,128]{2,1,0:T(8,128)(2,1)}), bf16[16,128,128]{2,1,0:T(8,128)(2,1)S(1)}, u32[]{:S(2)}, u32[]{:S(2)}) async-start(bf16[16,128,128]{2,1,0:T(8,128)(2,1)} %shard_map.86), calls=%async_computation.1 | async-start | bytes 1048576 | tf_op jit(solution)/shard_map/all_to_all | solution.py:348
  55.9 2.1 %copy-start = (bf16[36,256,256]{2,1,0:T(8,128)(2,1)}, bf16[36,256,256]{2,1,0:T(8,128)(2,1)S(1)}, u32[]{:S(2)}) copy-start(bf16[36,256,256]{2,1,0:T(8,128)(2,1)S(1)} %get-tuple-element.11.weights) | copy-start | bytes 14155780
  68.7 2.3 %copy-start.1 = (bf16[36,256,256]{2,1,0:T(8,128)(2,1)S(1)}, bf16[36,256,256]{2,1,0:T(8,128)(2,1)}, u32[]{:S(2)}) copy-start(bf16[36,256,256]{2,1,0:T(8,128)(2,1)} %copy-done) | copy-start | bytes 14155780

commit v2 on v1

--- a/solution.py
+++ b/solution.py
@@ -10,7 +10,17 @@
 
 HD = 128
 LOG2E = math.log2(math.e)
-VMEM_CAP = 16 * 1024 * 1024
+HBM = pl.BlockSpec(memory_space=pltpu.HBM)
+VMEM = pl.BlockSpec(memory_space=pltpu.VMEM)
+
+
+def far(array):
+    return pltpu.with_memory_space_constraint(array, pltpu.HBM)
+
+
+def near(array):
+    return pltpu.with_memory_space_constraint(array, pltpu.VMEM)
+VMEM_CAP = 12 * 1024 * 1024
 
 
 def call(body, out_shape, flops, moved, exps=0, **kwargs):
@@ -23,24 +33,34 @@
     )
 
 
-def split_kernel(pieces, per_piece, *refs):
-    *ins, out = refs
-    rows = ins[0].shape[0]
-    for place in range(pieces):
-        cols = slice(place * per_piece, (place + 1) * per_piece)
-        for which, ref in enumerate(ins):
-            out[place, which * rows : (which + 1) * rows, :] = ref[:, cols]
-
-
-def split_heads(arrays, pieces):
-    rows, width = arrays[0].shape
-    per_piece = width // pieces
-    return call(
-        functools.partial(split_kernel, pieces, per_piece),
-        jax.ShapeDtypeStruct((pieces, rows * len(arrays), per_piece), arrays[0].dtype),
+def run_copies(copies):
+    for copy in copies:
+        copy.start()
+    for copy in copies:
+        copy.wait()
+
+
+def join_kernel(source, out, done):
+    pieces, _, wide = source.shape
+    run_copies(
+        [
+            pltpu.make_async_copy(source.at[i], out.at[:, pl.ds(i * wide, wide)], done.at[i])
+            for i in range(pieces)
+        ]
+    )
+
+
+def join_heads(array):
+    pieces, rows, wide = array.shape
+    return call(
+        join_kernel,
+        pltpu.HBM((rows, pieces * wide), array.dtype),
         0,
-        4 * rows * width * len(arrays),
-    )(*arrays)
+        4 * rows * pieces * wide,
+        in_specs=[VMEM],
+        out_specs=HBM,
+        scratch_shapes=[pltpu.SemaphoreType.DMA((pieces,))],
+    )(array)
 
 
 def spread(ref, source, count, groups, pitch):
@@ -48,19 +68,60 @@
         ref[pl.ds(group, count, stride=pitch), :] = source[:, group * HD : (group + 1) * HD]
 
 
-def local_kernel(groups, pitch, gate, value, rates, weights, skip, out, summary, gated, decay, gain, direct):
+def first_kernel(groups, pitch, *refs):
+    gate_far, value_far, rates_far, weights_far, skip_far, query_far, key_far = refs[:7]
+    out, summary, pair = refs[7:10]
+    (gated, decay, gain, direct, gate, value, rates, weights, skip, query, key) = refs[10:21]
+    small, large, staged, moved = refs[21:]
     rows = gate.shape[0]
     poles = rates.shape[0]
+    parts = gate.shape[1] // large.shape[1]
+    pieces, _, wide = pair.shape
+    parameters = [
+        pltpu.make_async_copy(source, target, small.at[i])
+        for i, (source, target) in enumerate(
+            [(rates_far, rates), (weights_far, weights), (skip_far, skip)]
+        )
+    ]
+    streams = []
+    for i in range(large.shape[1]):
+        cols = pl.ds(i * parts, parts)
+        for which, (source, target) in enumerate([(gate_far, gate), (value_far, value)]):
+            streams.append(
+                pltpu.make_async_copy(source.at[:, cols], target.at[:, cols], large.at[which, i])
+            )
+    stages, moves = [], []
+    for which, (source, middle) in enumerate([(query_far, query), (key_far, key)]):
+        stages.append(pltpu.make_async_copy(source, middle, staged.at[which]))
+        for i in range(pieces):
+            cols = pl.ds(i * wide, wide)
+            moves.append(
+                pltpu.make_async_copy(
+                    middle.at[:, cols], pair.at[i, pl.ds(which * rows, rows)], moved.at[which, i]
+                )
+            )
+    for copy in parameters + streams + stages:
+        copy.start()
     if pitch != groups:
         for ref in (gated, decay, gain, direct):
             ref[...] = jnp.zeros_like(ref)
+    for copy in parameters:
+        copy.wait()
     spread(decay, jnp.exp(-rates[...]), poles, groups, pitch)
     spread(gain, weights[...] * jnp.sqrt(rates[...]), poles, groups, pitch)
     spread(direct, skip[...], 1, groups, pitch)
     for group in range(groups):
+        if group * HD % parts == 0:
+            for copy in streams[2 * (group * HD // parts) :][:2]:
+                copy.wait()
         cols = slice(group * HD, (group + 1) * HD)
         product = gate[:, cols].astype(jnp.float32) * value[:, cols].astype(jnp.float32)
         gated[pl.ds(group, rows, stride=pitch), :] = product
+
+    for copy in stages:
+        copy.wait()
+    for copy in moves:
+        copy.start()
 
     fades = [decay[m * pitch : (m + 1) * pitch, :] for m in range(poles)]
     gains = [gain[m * pitch : (m + 1) * pitch, :] for m in range(poles)]
@@ -80,31 +141,53 @@
     states = lax.fori_loop(0, rows, one, [zero] * poles, unroll=4)
     for m in range(poles):
         summary[m * pitch : (m + 1) * pitch, :] = states[m]
-
-
-def local_conv(gate, value, rates, weights, skip, pitch):
+    for copy in moves:
+        copy.wait()
+
+
+def first(gate, value, rates, weights, skip, query, key, pitch):
     rows, width = gate.shape
     poles = rates.shape[0]
+    heads = width // HD
+    streams = 4 if heads % 4 == 0 else 1
     f32 = jnp.float32
     return call(
-        functools.partial(local_kernel, width // HD, pitch),
+        functools.partial(first_kernel, heads, pitch),
         (
             jax.ShapeDtypeStruct((rows * pitch, HD), f32),
             jax.ShapeDtypeStruct((poles * pitch, HD), f32),
+            pltpu.HBM((heads, 2 * rows, HD), key.dtype),
         ),
         4 * poles * rows * width,
-        8 * rows * width,
+        16 * rows * width,
+        in_specs=[HBM] * 7,
+        out_specs=(VMEM, VMEM, HBM),
         scratch_shapes=[
             pltpu.VMEM((rows * pitch, HD), f32),
             pltpu.VMEM((poles * pitch, HD), f32),
             pltpu.VMEM((poles * pitch, HD), f32),
             pltpu.VMEM((pitch, HD), f32),
+            pltpu.VMEM((rows, width), gate.dtype),
+            pltpu.VMEM((rows, width), value.dtype),
+            pltpu.VMEM(rates.shape, f32),
+            pltpu.VMEM(weights.shape, f32),
+            pltpu.VMEM(skip.shape, f32),
+            pltpu.VMEM((rows, width), query.dtype),
+            pltpu.VMEM((rows, width), key.dtype),
+            pltpu.SemaphoreType.DMA((3,)),
+            pltpu.SemaphoreType.DMA((2, streams)),
+            pltpu.SemaphoreType.DMA((2,)),
+            pltpu.SemaphoreType.DMA((2, heads)),
         ],
-    )(gate, value, rates, weights, skip)
-
-
-def tail_kernel(groups, pitch, local, carry, rates, weights, gate, out, squares, full, decay, gain):
+    )(*map(far, (gate, value, rates, weights, skip, query, key)))
+
+
+def tail_kernel(
+    groups, pitch, local, carry, rates, weights, gate_far, out, squares, full, decay, gain, gate, done
+):
     rows = gate.shape[0]
+    fetch = pltpu.make_async_copy(gate_far, gate, done)
+    fetch.start()
     poles = rates.shape[0]
     if pitch != groups:
         for ref in (decay, gain):
@@ -124,6 +207,7 @@
         return states
 
     lax.fori_loop(0, rows, one, [gain[part, :] * carry[part, :] for part in parts], unroll=4)
+    fetch.wait()
     total = jnp.zeros((rows, HD), jnp.float32)
     for group in range(groups):
         cols = slice(group * HD, (group + 1) * HD)
@@ -151,14 +235,17 @@
             jax.ShapeDtypeStruct((width // HD, rows, HD), f32),
             jax.ShapeDtypeStruct((1, rows), f32),
         ),
-        3 * poles * rows * width,
+        4700 * poles * rows * width,
         10 * rows * width,
+        in_specs=[VMEM, VMEM, VMEM, VMEM, HBM],
         scratch_shapes=[
             pltpu.VMEM((rows * pitch, HD), f32),
             pltpu.VMEM((poles * pitch, HD), f32),
             pltpu.VMEM((poles * pitch, HD), f32),
+            pltpu.VMEM((rows, width), gate.dtype),
+            pltpu.SemaphoreType.DMA,
         ],
-    )(local, carry, rates, weights, gate)
+    )(local, carry, rates, weights, far(gate))
 
 
 def norm_kernel(channels, conv, squares, out):
@@ -185,42 +272,49 @@
     size = lax.axis_size(axis)
     place = lax.axis_index(axis)
     span = rates * jnp.float32(block_rows)
-    total, before = summary, jnp.zeros_like(summary)
-    step = 1
-    while step < size:
-        many = min(4, size // step)
-        mine = place // step % many
-        inside = place % step
-        others = [
-            lax.ppermute(total, axis, [(i, i ^ (step * k)) for i in range(size)])
-            for k in range(1, many)
-        ]
-        new_total = jnp.exp(-span * (step * (many - 1 - mine)).astype(jnp.float32)) * total
-        for k, other in enumerate(others, 1):
-            its = mine ^ k
-            gap = ((mine - 1 - its) * step + inside).astype(jnp.float32)
-            fade = jnp.exp(-span * jnp.maximum(gap, 0.0))
-            before = before + jnp.where(its < mine, fade * other, 0.0)
-            fade = jnp.exp(-span * (step * (many - 1 - its)).astype(jnp.float32))
-            new_total = new_total + fade * other
-        total = new_total
-        step *= many
+
+    def fade(blocks):
+        return jnp.exp(-span * jnp.maximum(blocks, 0).astype(jnp.float32))
+
+    strides = [1]
+    while strides[-1] * 4 < size:
+        strides.append(strides[-1] * 4)
+    before, above = None, size
+    for stride in reversed(strides):
+        many = above // stride
+        digit, inside = place // stride % many, place % above
+        total = None if before is None else fade(digit * stride) * before
+        for k in range(1, many):
+            other = digit ^ k
+            gap = other * stride - inside - 1
+            sent = summary
+            if before is not None:
+                sent = fade(other * stride) * before + jnp.where(
+                    digit < other, fade(gap) * summary, 0.0
+                )
+            got = lax.ppermute(sent, axis, [(i, i ^ (stride * k)) for i in range(size)])
+            if before is None:
+                gap = digit * stride - (inside - digit * stride + other * stride) - 1
+                got = jnp.where(other < digit, fade(gap) * got, 0.0)
+            total = got if total is None else total + got
+        before, above = total, stride
     return before
 
 
-def score_kernel(block, inputs, weights, totals, scores):
-    chunks, twice, _ = inputs.shape
+def score_kernel(block, pair, weights, totals, scores, packed, sent):
+    chunks, twice, _ = pair.shape
     rows = twice // 2
     per_block = block // rows
     factor = LOG2E * HD ** (-0.5)
     row = lax.broadcasted_iota(jnp.int32, (block, block), 0)
     col = lax.broadcasted_iota(jnp.int32, (block, block), 1)
     visible = col <= row
+    sending = []
     for turn in range(chunks // per_block):
-        query = inputs[turn * per_block : (turn + 1) * per_block, 0:rows, :].reshape(block, HD)
+        query = pair[turn * per_block : (turn + 1) * per_block, 0:rows].reshape(block, HD)
         top = None
         for part in range(turn + 1):
-            key = inputs[part * per_block : (part + 1) * per_block, rows:, :].reshape(block, HD)
+            key = pair[part * per_block : (part + 1) * per_block, rows:].reshape(block, HD)
             got = lax.dot_general(
                 query, key, (((1,), (1,)), ((), ())), preferred_element_type=jnp.float32
             )
@@ -232,24 +326,36 @@
                 top = one if top is None else jnp.maximum(top, one)
         top = jnp.max(top, axis=1, keepdims=True) * factor
         summed = jnp.zeros((block, HD), jnp.float32)
+        first = turn * (turn + 1) // 2
         for part in range(turn + 1):
             expo = jnp.exp2(scores[:, part * block : (part + 1) * block] * factor - top)
             for lane in range(0, block, HD):
                 summed = summed + expo[:, lane : lane + HD]
-            weights[turn * (turn + 1) // 2 + part] = expo.astype(jnp.bfloat16)
+            packed[first + part] = expo.astype(jnp.bfloat16)
         total = jnp.sum(summed, axis=1, keepdims=True)
         totals[turn * block : (turn + 1) * block, :] = jnp.broadcast_to(total, (block, HD))
-
-
-def mix_kernel(block, weights, totals, values, out):
+        tiles = pl.ds(first, turn + 1)
+        sending.append(pltpu.make_async_copy(packed.at[tiles], weights.at[tiles], sent.at[turn]))
+        sending[-1].start()
+    for copy in sending:
+        copy.wait()
+
+
+def mix_kernel(block, weights, totals, values, out, packed, got):
     chunks, rows, _ = values.shape
     per_block = block // rows
+    coming = []
     for turn in range(chunks // per_block):
+        tiles = pl.ds(turn * (turn + 1) // 2, turn + 1)
+        coming.append(pltpu.make_async_copy(weights.at[tiles], packed.at[tiles], got.at[turn]))
+        coming[-1].start()
+    for turn in range(chunks // per_block):
+        coming[turn].wait()
         mixed = jnp.zeros((block, HD), jnp.float32)
         for part in range(turn + 1):
             value = values[part * per_block : (part + 1) * per_block].reshape(block, HD)
             mixed = mixed + jnp.dot(
-                weights[turn * (turn + 1) // 2 + part], value, preferred_element_type=jnp.float32
+                packed[turn * (turn + 1) // 2 + part], value, preferred_element_type=jnp.float32
             )
         mixed = mixed / totals[turn * block : (turn + 1) * block, :]
         out[turn * per_block : (turn + 1) * per_block] = mixed.astype(out.dtype).reshape(
@@ -266,19 +372,26 @@
 
 def head_weights(pair):
     chunks, twice, _ = pair.shape
-    length = chunks * twice // 2
-    block = block_of(chunks, twice // 2)
-    tiles = (length // block) * (length // block + 1) // 2
+    rows = twice // 2
+    length = chunks * rows
+    block = block_of(chunks, rows)
+    turns = length // block
+    tiles = turns * (turns + 1) // 2
     return call(
         functools.partial(score_kernel, block),
         (
-            jax.ShapeDtypeStruct((tiles, block, block), jnp.bfloat16),
+            pltpu.HBM((tiles, block, block), jnp.bfloat16),
             jax.ShapeDtypeStruct((length, HD), jnp.float32),
         ),
         tiles * block * block * (2 * HD + 8),
         tiles * block * block * 2,
         tiles * block * block,
-        scratch_shapes=[pltpu.VMEM((block, length), jnp.float32)],
+        out_specs=(HBM, VMEM),
+        scratch_shapes=[
+            pltpu.VMEM((block, length), jnp.float32),
+            pltpu.VMEM((tiles, block, block), jnp.bfloat16),
+            pltpu.SemaphoreType.DMA((turns,)),
+        ],
     )(pair)
 
 
@@ -290,7 +403,12 @@
         jax.ShapeDtypeStruct((chunks, rows, HD), jnp.bfloat16),
         weights.size * 2 * HD,
         weights.size * 2,
-    )(weights, totals, values)
+        in_specs=[HBM, VMEM, VMEM],
+        scratch_shapes=[
+            pltpu.VMEM(weights.shape, weights.dtype),
+            pltpu.SemaphoreType.DMA((chunks * rows // block,)),
+        ],
+    )(far(weights), totals, values)
 
 
 def gathered_head(query, key, value, first_row):
@@ -337,10 +455,10 @@
     )
     pitch = -(-heads // 8) * 8
 
-    pair = exchange(split_heads([query_rows, key_rows], heads))
-    part, summary = local_conv(
-        gate_inner, value_in, pole_rates, pole_weights, skip_gain[None, :], pitch
-    )
+    part, summary, chunks = first(
+        gate_inner, value_in, pole_rates, pole_weights, skip_gain[None, :], query_rows, key_rows, pitch
+    )
+    pair = exchange(chunks)
     spread_rates = pole_rates.reshape(-1, heads, HD)
     spread_rates = jnp.pad(spread_rates, ((0, 0), (0, pitch - heads), (0, 0))).reshape(-1, HD)
     carry = prefix_state(summary, spread_rates, rows, "seq")
@@ -362,7 +480,7 @@
             gather(values.reshape(span, HD)),
             mine * span,
         ).reshape(heads, rows, HD)
-    return jnp.transpose(exchange(mixed), (1, 0, 2)).reshape(rows, width)
+    return join_heads(exchange(mixed))
 
 
 def solution(mesh):

time: 92.6 us -> 82.9 us (0.90)
  local copies, waits for them, and re-layouts: 13.6 us -> 2.4 us
  Pallas kernels: 9.37 us -> 14.3 us
  waiting for transfers between devices: 27.1 us -> 22.6 us
  starting transfers between devices: 20.9 us -> 22 us
    ppermute x6, waiting for transfers between devices: 16.4 us -> 6.52 us  [prefix_state(): got = lax.ppermute(sent, axis, [(i, i ^ stride * k) for i in range(size)])]
    unnamed x24 -> x8, local copies, waits for them, and re-layouts: 12.1 us -> 2.22 us
    all_to_all x1, waiting for transfers between devices: 0.01 us -> 5.88 us  [local(): pair = exchange(chunks)]
    pallas_call x3, Pallas kernels: 5.8 us -> 8.18 us  [the longest x1 3.71 us: first(): call(functools.partial(first_kernel, heads, pitch), (jax.ShapeDtypeStruct...]
    pallas_call x1, Pallas kernels: 1.38 us -> 3.53 us  [head_mix(): call(functools.partial(mix_kernel, block), jax.ShapeDtypeStruct((chunks,...]
    all_to_all x1, starting transfers between devices: 8.31 us -> 7.08 us  [local(): pair = exchange(chunks)]
    all_to_all x1, starting transfers between devices: 4.59 us -> 5.77 us  [local(): exchange(normalize(conv, lax.psum(squares, 'chan'), channels, heads))]
    ppermute x6, starting transfers between devices: 8 us -> 9.17 us  [prefix_state(): got = lax.ppermute(sent, axis, [(i, i ^ stride * k) for i in range(size)])]
  transfers between devices with their start and end apart: 8 -> 8, of which waited for: 5 -> 3; matrix products, arithmetic and copies ran while one was open for 0% -> 1% of each run, Pallas kernels for 7% -> 7%
where the time goes in v2:
time: 82.9 us; the launch traced here: 82.4 us
  waiting for transfers between devices  22.6 us (27%)
  starting transfers between devices  22 us (27%)
  blocking collectives  19.8 us (24%)
  Pallas kernels  14.3 us (17%)
  local copies, waits for them, and re-layouts  2.4 us (3%)
  other arithmetic  1.03 us (1%)
    all_to_all x1, blocking collectives, local(): return join_heads(exchange(mixed))  17.4 us
    all_to_all x1, waiting for transfers between devices, local(): exchange(normalize(conv, lax.psum(squares, 'chan'), channels, heads))  10.2 us
    ppermute x6, starting transfers between devices, prefix_state(): got = lax.ppermute(sent, axis, [(i, i ^ stride * k) for i in range(size)])  9.17 us
    all_to_all x1, starting transfers between devices, local(): pair = exchange(chunks)  7.08 us
    ppermute x6, waiting for transfers between devices, prefix_state(): got = lax.ppermute(sent, axis, [(i, i ^ stride * k) for i in range(size)])  6.52 us
    all_to_all x1, waiting for transfers between devices, local(): pair = exchange(chunks)  5.88 us
    all_to_all x1, starting transfers between devices, local(): exchange(normalize(conv, lax.psum(squares, 'chan'), channels, heads))  5.77 us
    pallas_call x1, Pallas kernels, first(): call(functools.partial(first_kernel, heads, pitch), (jax.ShapeDtypeStruct...  3.71 us
  transfers between devices with their start and end apart: 8, of which 3 were waited for; matrix products, arithmetic and copies ran while one was open for 1% of the time, Pallas kernels for 7%

profile of v2, /device:TPU:0, one launch (start us, length us, event | category | flops | bytes accessed | tf_op | source)
XLA Modules:
  0.0 82.4 jit_solution(8433734025825278823)
XLA Ops:
  0.0 0.0 copy-start
  0.0 3.7 %shard_map.82 = (f32[2048,128]{1,0:T(8,128)S(1)}, f32[128,128]{1,0:T(8,128)S(1)}, bf16[16,256,128]{2,1,0:T(8,128)(2,1)}) custom-call(bf16[128,2048]{1,0:T(8,128)(2,1)} %refs_0_.1, bf16[128,2048]{1,0:T(8,128)(2,1)} %refs_1_.1, f32[8,2048]{1,0:T(8,128)} %rates.1, f32[8,2048]{1,0:T(8,128)} %weights.1, f32[1,2048]{1,0:T(1,128)} %bitcast.1, ...), custom_call_target="tpu_custom_call" | custom-call | flops 8388608 | bytes 4194304 | tf_op jit(solution)/shard_map/pallas_call | solution.py:154
  3.7 0.0 copy-start.2
  3.7 1.0 %copy-done.2 = f32[2048,128]{1,0:T(8,128)} copy-done((f32[2048,128]{1,0:T(8,128)}, f32[2048,128]{1,0:T(8,128)S(1)}, u32[]{:S(2)}) %copy-start.2) | copy-done | bytes 1048600
  4.7 5.0 %collective-permute-start.2 = (f32[128,128]{1,0:T(8,128)S(1)}, f32[128,128]{1,0:T(8,128)S(1)}, u32[]{:S(2)}, u32[]{:S(2)}) collective-permute-start(f32[128,128]{1,0:T(8,128)S(1)} %get-tuple-element.16), channel_id=1, source_target_pairs={{0,24},{2,26},{4,28},{6,30},{8,16},{10,18},{12,20},{14,22},{16,8},... | collective-permute-start | bytes 196616 | tf_op jit(solution)/shard_map/ppermute | solution.py:295
  9.8 0.0 collective-permute-start.1
  9.8 0.6 collective-permute-start
  10.3 7.1 %all-to-all-start = ((bf16[16,256,128]{2,1,0:T(8,128)(2,1)}), bf16[16,256,128]{2,1,0:T(8,128)(2,1)S(1)}, u32[]{:S(2)}, u32[]{:S(2)}) async-start(bf16[16,256,128]{2,1,0:T(8,128)(2,1)} %get-tuple-element.12), calls=%async_computation | async-start | bytes 2097152 | tf_op jit(solution)/shard_map/all_to_all | solution.py:461
  17.5 0.9 %multiply_exponential_fusion.9 = (f32[8,2048]{1,0:T(8,128)S(1)}, f32[8,2048]{1,0:T(8,128)S(1)}, f32[8,2048]{1,0:T(8,128)S(1)}, f32[8,2048]{1,0:T(8,128)S(1)}, f3...) fusion(f32[]{:T(128)S(6)} %convert_element_type.30, ...), kind=kLoop, calls=%fused_computation.14 | loop fusion | flops 196608 | bytes 720936 | tf_op jit(solution)/shard_map/exp | solution.py:277
  18.7 0.0 collective-permute-done.2
  18.7 0.0 collective-permute-done.1
  18.7 0.0 collective-permute-done
  18.8 1.9 %collective-permute-start.4 = (f32[128,128]{1,0:T(8,128)S(1)}, f32[128,128]{1,0:T(8,128)S(1)}, u32[]{:S(2)}, u32[]{:S(2)}) collective-permute-start(f32[128,128]{1,0:T(8,128)S(1)} %get-tuple-element.21), channel_id=1, source_target_pairs={{0,4},{2,6},{4,0},{6,2},{8,12},{10,14},{12,8},{14,10},{16,20},{18,... | collective-permute-start | bytes 196616 | tf_op jit(solution)/shard_map/ppermute | solution.py:295
  20.7 1.5 %collective-permute-start.5 = (f32[128,128]{1,0:T(8,128)S(1)}, f32[128,128]{1,0:T(8,128)S(1)}, u32[]{:S(2)}, u32[]{:S(2)}) collective-permute-start(f32[128,128]{1,0:T(8,128)S(1)} %get-tuple-element.22), channel_id=1, source_target_pairs={{0,6},{2,4},{4,2},{6,0},{8,14},{10,12},{12,10},{14,8},{16,22},{18,... | collective-permute-start | bytes 196616 | tf_op jit(solution)/shard_map/ppermute | solution.py:295
  22.2 0.2 collective-permute-start.3
  22.4 6.5 %collective-permute-done.4 = f32[128,128]{1,0:T(8,128)S(1)} collective-permute-done((f32[128,128]{1,0:T(8,128)S(1)}, f32[128,128]{1,0:T(8,128)S(1)}, u32[]{:S(2)}, u32[]{:S(2)}) %collective-permute-start.4) | collective-permute-done | bytes 65568 | tf_op jit(solution)/shard_map/ppermute | solution.py:295
  28.9 0.0 collective-permute-done.5
  28.9 0.0 collective-permute-done.3
  28.9 0.0 copy-done
  29.0 0.0 copy-done.1
  29.0 0.0 copy-start.3
  29.0 1.2 %copy-done.3 = f32[2048,128]{1,0:T(8,128)S(1)} copy-done((f32[2048,128]{1,0:T(8,128)S(1)}, f32[2048,128]{1,0:T(8,128)}, u32[]{:S(2)}) %copy-start.3) | copy-done | bytes 1048600
  30.2 1.6 %shard_map.84 = (f32[16,128,128]{2,1,0:T(8,128)S(1)}, f32[1,128]{1,0:T(1,128)S(1)}) custom-call(f32[2048,128]{1,0:T(8,128)S(1)} %copy-done.3, f32[128,128]{1,0:T(8,128)S(1)} %add_add_fusion.carry, f32[8,2048]{1,0:T(8,128)S(1)} %copy-done, f32[8,2048]{1,0:T(8,128)S(1)} %copy-done.1, bf16[128,2048]{1,0:T(8,128)(2,1)} %gate_far.1), custom_call_target="tpu_custom_call" | custom-call | flops 9856614400 | bytes 2621440 | tf_op jit(solution)/shard_map/pallas_call | solution.py:232
  31.8 2.5 %psum.7.squares = f32[1,128]{1,0:T(1,128)S(1)} all-reduce(f32[1,128]{1,0:T(1,128)S(1)} %get-tuple-element.18), channel_id=1, replica_groups=mesh['seq'=16,'chan'=2] {'chan'}, use_global_device_ids=true, to_apply=%region_0.1 | all-reduce | flops 128 | bytes 1024 | tf_op jit(solution)/shard_map/psum | solution.py:466
  34.3 1.0 %shard_map.85 = bf16[16,128,128]{2,1,0:T(8,128)(2,1)} custom-call(f32[16,128,128]{2,1,0:T(8,128)S(1)} %get-tuple-element.17.conv, f32[1,128]{1,0:T(1,128)S(1)} %psum.7.squares), custom_call_target="tpu_custom_call" | custom-call | flops 262144 | bytes 1572864 | tf_op jit(solution)/shard_map/pallas_call | solution.py:263
  35.2 5.9 %all-to-all-done.pair = bf16[16,256,128]{2,1,0:T(8,128)(2,1)S(1)} async-done(((bf16[16,256,128]{2,1,0:T(8,128)(2,1)}), bf16[16,256,128]{2,1,0:T(8,128)(2,1)S(1)}, u32[]{:S(2)}, u32[]{:S(2)}) %all-to-all-start) | async-done | bytes 1048608 | tf_op jit(solution)/shard_map/all_to_all | solution.py:461
  41.1 5.8 %all-to-all-start.1 = ((bf16[16,128,128]{2,1,0:T(8,128)(2,1)}), bf16[16,128,128]{2,1,0:T(8,128)(2,1)S(1)}, u32[]{:S(2)}, u32[]{:S(2)}) async-start(bf16[16,128,128]{2,1,0:T(8,128)(2,1)} %shard_map.85), calls=%async_computation.1 | async-start | bytes 1048576 | tf_op jit(solution)/shard_map/all_to_all | solution.py:466
  46.9 3.6 %shard_map.83 = (bf16[36,256,256]{2,1,0:T(8,128)(2,1)}, f32[2048,128]{1,0:T(8,128)S(1)}) custom-call(bf16[16,256,128]{2,1,0:T(8,128)(2,1)S(1)} %all-to-all-done.pair), custom_call_target="tpu_custom_call" | custom-call | flops 622854144 | bytes 4718592 | tf_op jit(solution)/shard_map/pallas_call | solution.py:380
  50.4 10.2 %all-to-all-done.1.values = bf16[16,128,128]{2,1,0:T(8,128)(2,1)S(1)} async-done(((bf16[16,128,128]{2,1,0:T(8,128)(2,1)}), bf16[16,128,128]{2,1,0:T(8,128)(2,1)S(1)}, u32[]{:S(2)}, u32[]{:S(2)}) %all-to-all-start.1) | async-done | bytes 524320 | tf_op jit(solution)/shard_map/all_to_all | solution.py:466
  60.6 3.5 %shard_map.86 = bf16[16,128,128]{2,1,0:T(8,128)(2,1)S(1)} custom-call(bf16[36,256,256]{2,1,0:T(8,128)(2,1)} %get-tuple-element.13.weights, f32[2048,128]{1,0:T(8,128)S(1)} %get-tuple-element.14.totals, bf16[16,128,128]{2,1,0:T(8,128)(2,1)S(1)} %all-to-all-done.1.values), custom_call_target="tpu_custom_call" | custom-call | flops 603979776 | bytes 4718592 | tf_op jit(solution)/shard_map/pallas_call | solution.py:401
  64.1 17.4 %all_to_all.15.source = bf16[16,128,128]{2,1,0:T(8,128)(2,1)S(1)} all-to-all(bf16[16,128,128]{2,1,0:T(8,128)(2,1)S(1)} %shard_map.86), channel_id=1, replica_groups=mesh['seq'=16,'chan'=2] {'seq'}, dimensions={0} | all-to-all | bytes 1048576 | tf_op jit(solution)/shard_map/all_to_all | solution.py:483
  81.5 0.9 %shard_map.87 = bf16[128,2048]{1,0:T(8,128)(2,1)} custom-call(bf16[16,128,128]{2,1,0:T(8,128)(2,1)S(1)} %all_to_all.15.source), custom_call_target="tpu_custom_call" | custom-call | bytes 1048576 | tf_op jit(solution)/shard_map/pallas_call | solution.py:55
  (14 shorter events, 0.3 us)
Async XLA Ops:
  0.0 29.0 %copy-start = (f32[8,2048]{1,0:T(8,128)S(1)}, f32[8,2048]{1,0:T(8,128)}, u32[]{:S(2)}) copy-start(f32[8,2048]{1,0:T(8,128)} %rates.1) | copy-start | bytes 196612
  0.0 29.0 %copy-start.1 = (f32[8,2048]{1,0:T(8,128)S(1)}, f32[8,2048]{1,0:T(8,128)}, u32[]{:S(2)}) copy-start(f32[8,2048]{1,0:T(8,128)} %weights.1) | copy-start | bytes 196612
  3.7 1.0 %copy-start.2 = (f32[2048,128]{1,0:T(8,128)}, f32[2048,128]{1,0:T(8,128)S(1)}, u32[]{:S(2)}) copy-start(f32[2048,128]{1,0:T(8,128)S(1)} %get-tuple-element.15.local) | copy-start | bytes 3145732
  4.7 14.0 %collective-permute-start.2 = (f32[128,128]{1,0:T(8,128)S(1)}, f32[128,128]{1,0:T(8,128)S(1)}, u32[]{:S(2)}, u32[]{:S(2)}) collective-permute-start(f32[128,128]{1,0:T(8,128)S(1)} %get-tuple-element.16), channel_id=1, source_target_pairs={{0,24},{2,26},{4,28},{6,30},{8,16},{10,18},{12,20},{14,22},{16,8},... | collective-permute-start | bytes 196616 | tf_op jit(solution)/shard_map/ppermute | solution.py:295
  9.8 9.0 %collective-permute-start.1 = (f32[128,128]{1,0:T(8,128)S(1)}, f32[128,128]{1,0:T(8,128)S(1)}, u32[]{:S(2)}, u32[]{:S(2)}) collective-permute-start(f32[128,128]{1,0:T(8,128)S(1)} %get-tuple-element.16), channel_id=1, source_target_pairs={{0,16},{2,18},{4,20},{6,22},{8,24},{10,26},{12,28},{14,30},{16,0},... | collective-permute-start | bytes 196616 | tf_op jit(solution)/shard_map/ppermute | solution.py:295
  9.8 9.0 %collective-permute-start = (f32[128,128]{1,0:T(8,128)S(1)}, f32[128,128]{1,0:T(8,128)S(1)}, u32[]{:S(2)}, u32[]{:S(2)}) collective-permute-start(f32[128,128]{1,0:T(8,128)S(1)} %get-tuple-element.16), channel_id=1, source_target_pairs={{0,8},{2,10},{4,12},{6,14},{8,0},{10,2},{12,4},{14,6},{16,24},{18,... | collective-permute-start | bytes 196616 | tf_op jit(solution)/shard_map/ppermute | solution.py:295
  10.3 30.8 %all-to-all-start = ((bf16[16,256,128]{2,1,0:T(8,128)(2,1)}), bf16[16,256,128]{2,1,0:T(8,128)(2,1)S(1)}, u32[]{:S(2)}, u32[]{:S(2)}) async-start(bf16[16,256,128]{2,1,0:T(8,128)(2,1)} %get-tuple-element.12), calls=%async_computation | async-start | bytes 2097152 | tf_op jit(solution)/shard_map/all_to_all | solution.py:461
  18.8 10.1 %collective-permute-start.4 = (f32[128,128]{1,0:T(8,128)S(1)}, f32[128,128]{1,0:T(8,128)S(1)}, u32[]{:S(2)}, u32[]{:S(2)}) collective-permute-start(f32[128,128]{1,0:T(8,128)S(1)} %get-tuple-element.21), channel_id=1, source_target_pairs={{0,4},{2,6},{4,0},{6,2},{8,12},{10,14},{12,8},{14,10},{16,20},{18,... | collective-permute-start | bytes 196616 | tf_op jit(solution)/shard_map/ppermute | solution.py:295
  20.7 8.2 %collective-permute-start.5 = (f32[128,128]{1,0:T(8,128)S(1)}, f32[128,128]{1,0:T(8,128)S(1)}, u32[]{:S(2)}, u32[]{:S(2)}) collective-permute-start(f32[128,128]{1,0:T(8,128)S(1)} %get-tuple-element.22), channel_id=1, source_target_pairs={{0,6},{2,4},{4,2},{6,0},{8,14},{10,12},{12,10},{14,8},{16,22},{18,... | collective-permute-start | bytes 196616 | tf_op jit(solution)/shard_map/ppermute | solution.py:295
  22.2 6.7 %collective-permute-start.3 = (f32[128,128]{1,0:T(8,128)S(1)}, f32[128,128]{1,0:T(8,128)S(1)}, u32[]{:S(2)}, u32[]{:S(2)}) collective-permute-start(f32[128,128]{1,0:T(8,128)S(1)} %get-tuple-element.19), channel_id=1, source_target_pairs={{0,2},{2,0},{4,6},{6,4},{8,10},{10,8},{12,14},{14,12},{16,18},{18,... | collective-permute-start | bytes 196616 | tf_op jit(solution)/shard_map/ppermute | solution.py:295
  29.0 1.2 %copy-start.3 = (f32[2048,128]{1,0:T(8,128)S(1)}, f32[2048,128]{1,0:T(8,128)}, u32[]{:S(2)}) copy-start(f32[2048,128]{1,0:T(8,128)} %copy-done.2) | copy-start | bytes 3145732
  41.1 19.5 %all-to-all-start.1 = ((bf16[16,128,128]{2,1,0:T(8,128)(2,1)}), bf16[16,128,128]{2,1,0:T(8,128)(2,1)S(1)}, u32[]{:S(2)}, u32[]{:S(2)}) async-start(bf16[16,128,128]{2,1,0:T(8,128)(2,1)} %shard_map.85), calls=%async_computation.1 | async-start | bytes 1048576 | tf_op jit(solution)/shard_map/all_to_all | solution.py:466

commit v3 on v2

v3 whole, which is shorter than its diff:
```python
import functools
import math

import jax
import jax.numpy as jnp
from jax import lax
from jax.experimental import pallas as pl
from jax.experimental.pallas import tpu as pltpu
from jax.sharding import PartitionSpec as P

HD = 128
LOG2E = math.log2(math.e)
PLANE = 4
HBM = pl.BlockSpec(memory_space=pltpu.HBM)
VMEM = pl.BlockSpec(memory_space=pltpu.VMEM)


def far(array):
    return pltpu.with_memory_space_constraint(array, pltpu.HBM)


def near(array):
    return pltpu.with_memory_space_constraint(array, pltpu.VMEM)
VMEM_CAP = 12 * 1024 * 1024


def call(body, out_shape, flops, moved, exps=0, **kwargs):
    return pl.pallas_call(
        body,
        out_shape=out_shape,
        compiler_params=pltpu.CompilerParams(vmem_limit_bytes=VMEM_CAP),
        cost_estimate=pl.CostEstimate(flops=flops, bytes_accessed=moved, transcendentals=exps),
        **kwargs,
    )


def run_copies(copies):
    for copy in copies:
        copy.start()
    for copy in copies:
        copy.wait()


def join_kernel(source, out, done):
    pieces, _, wide = source.shape
    run_copies(
        [
            pltpu.make_async_copy(source.at[i], out.at[:, pl.ds(i * wide, wide)], done.at[i])
            for i in range(pieces)
        ]
    )


def join_heads(array):
    pieces, rows, wide = array.shape
    return call(
        join_kernel,
        pltpu.HBM((rows, pieces * wide), array.dtype),
        0,
        4 * rows * pieces * wide,
        in_specs=[VMEM],
        out_specs=HBM,
        scratch_shapes=[pltpu.SemaphoreType.DMA((pieces,))],
    )(array)


def spread(ref, source, count, groups, pitch):
    for group in range(groups):
        ref[pl.ds(group, count, stride=pitch), :] = source[:, group * HD : (group + 1) * HD]


def first_kernel(groups, pitch, *refs):
    gate_far, value_far, rates_far, weights_far, skip_far, query_far, key_far = refs[:7]
    kept, summary, spread_rates, gain, direct, pair = refs[7:13]
    gated, gate, value, rates, weights, skip, query, key, held = refs[13:22]
    small, large, staged, moved, keep = refs[22:]
    rows = gate.shape[0]
    poles = rates.shape[0]
    parts = gate.shape[1] // large.shape[1]
    pieces, _, wide = pair.shape
    parameters = [
        pltpu.make_async_copy(source, target, small.at[i])
        for i, (source, target) in enumerate(
            [(rates_far, rates), (weights_far, weights), (skip_far, skip)]
        )
    ]
    streams = []
    for i in range(large.shape[1]):
        cols = pl.ds(i * parts, parts)
        for which, (source, target) in enumerate([(gate_far, gate), (value_far, value)]):
            streams.append(
                pltpu.make_async_copy(source.at[:, cols], target.at[:, cols], large.at[which, i])
            )
    splits = []
    for which, (source, middle) in enumerate([(query_far, query), (key_far, key)]):
        at = pl.ds(which * rows, rows)
        stage = pltpu.make_async_copy(source, middle, staged.at[which])
        move = pltpu.make_async_copy(held.at[:, at], pair.at[:, at], moved.at[which])
        splits.append((stage, middle, which * rows, move))
    for copy in parameters + [splits[0][0]] + streams + [splits[1][0]]:
        copy.start()
    if pitch != groups:
        for ref in (gated, spread_rates, gain, direct):
            ref[...] = jnp.zeros_like(ref)
    for stage, middle, row, move in splits[:1]:
        stage.wait()
        for i in range(pieces):
            held[i, row : row + rows, :] = middle[:, i * wide : (i + 1) * wide]
        move.start()
    for copy in parameters:
        copy.wait()
    spread(spread_rates, rates[...], poles, groups, pitch)
    spread(gain, weights[...] * jnp.sqrt(rates[...]), poles, groups, pitch)
    spread(direct, skip[...], 1, groups, pitch)
    for group in range(groups):
        if group * HD % parts == 0:
            for copy in streams[2 * (group * HD // parts) :][:2]:
                copy.wait()
        cols = slice(group * HD, (group + 1) * HD)
        product = gate[:, cols].astype(jnp.float32) * value[:, cols].astype(jnp.float32)
        gated[pl.ds(group, rows, stride=pitch), :] = product
    keeping = pltpu.make_async_copy(gated, kept, keep)
    keeping.start()
    for stage, middle, row, move in splits[1:]:
        stage.wait()
        for i in range(pieces):
            held[i, row : row + rows, :] = middle[:, i * wide : (i + 1) * wide]
        move.start()

    slots = [slice(m * pitch, (m + 1) * pitch) for m in range(poles)]
    fades = [jnp.exp(-spread_rates[slot, :]) for slot in slots]

    def one(t, states):
        now = gated[pl.ds(pl.multiple_of(t * pitch, pitch), pitch), :]
        return [fade * state + now for fade, state in zip(fades, states)]

    zero = jnp.zeros((pitch, HD), jnp.float32)
    states = lax.fori_loop(0, rows, one, [zero] * poles, unroll=8)
    for slot, state in zip(slots, states):
        summary[slot, :] = state
    for stage, middle, row, move in splits:
        move.wait()
    keeping.wait()


def first(gate, value, rates, weights, skip, query, key, pitch):
    rows, width = gate.shape
    poles = rates.shape[0]
    heads = width // HD
    streams = 2 if heads % 2 == 0 else 1
    f32 = jnp.float32
    return call(
        functools.partial(first_kernel, heads, pitch),
        (
            pltpu.HBM((rows * pitch, HD), f32),
            jax.ShapeDtypeStruct((poles * pitch, HD), f32),
            jax.ShapeDtypeStruct((poles * pitch, HD), f32),
            jax.ShapeDtypeStruct((poles * pitch, HD), f32),
            jax.ShapeDtypeStruct((pitch, HD), f32),
            pltpu.HBM((heads, 2 * rows, HD), key.dtype),
        ),
        2 * poles * rows * width,
        16 * rows * width,
        in_specs=[HBM] * 7,
        out_specs=(HBM, VMEM, VMEM, VMEM, VMEM, HBM),
        scratch_shapes=[
            pltpu.VMEM((rows * pitch, HD), f32),
            pltpu.VMEM((rows, width), gate.dtype),
            pltpu.VMEM((rows, width), value.dtype),
            pltpu.VMEM(rates.shape, f32),
            pltpu.VMEM(weights.shape, f32),
            pltpu.VMEM(skip.shape, f32),
            pltpu.VMEM((rows, width), query.dtype),
            pltpu.VMEM((rows, width), key.dtype),
            pltpu.VMEM((heads, 2 * rows, HD), key.dtype),
            pltpu.SemaphoreType.DMA((3,)),
            pltpu.SemaphoreType.DMA((2, streams)),
            pltpu.SemaphoreType.DMA((2,)),
            pltpu.SemaphoreType.DMA((2,)),
            pltpu.SemaphoreType.DMA,
        ],
    )(*map(far, (gate, value, rates, weights, skip, query, key)))


def tail_kernel(groups, pitch, kept, carry, rates, gain, direct, gate_far, *refs):
    out, squares, gated, full, gate, come, done = refs
    rows = gate.shape[0]
    runs = come.shape[0]
    run = rows // runs
    streams = []
    for i in range(runs):
        at = pl.ds(i * run * pitch, run * pitch)
        streams.append(pltpu.make_async_copy(kept.at[at], gated.at[at], come.at[i]))
        streams[-1].start()
    fetch = pltpu.make_async_copy(gate_far, gate, done)
    fetch.start()
    slots = [slice(first, first + pitch) for first in range(0, rates.shape[0], pitch)]
    fades = [jnp.exp(-rates[slot, :]) for slot in slots]
    gains = [gain[slot, :] for slot in slots]
    own = direct[...]

    def one(t, states):
        at = pl.ds(pl.multiple_of(t * pitch, pitch), pitch)
        now = gated[at, :]
        states = [fade * state + now for fade, state in zip(fades, states)]
        terms = [own * now] + [g * state for g, state in zip(gains, states)]
        while len(terms) > 1:
            terms = [a + b for a, b in zip(terms[::2], terms[1::2])] + terms[len(terms) // 2 * 2 :]
        full[at, :] = terms[0]
        return states

    states = [carry[slot, :] for slot in slots]
    for i, stream in enumerate(streams):
        stream.wait()
        states = lax.fori_loop(i * run, (i + 1) * run, one, states, unroll=4)
    fetch.wait()
    total = jnp.zeros((rows, HD), jnp.float32)
    for group in range(groups):
        cols = slice(group * HD, (group + 1) * HD)
        conv = gate[:, cols].astype(jnp.float32) * full[pl.ds(group, rows, stride=pitch), :]
        out[group] = conv
        total = total + conv * conv
    ones = jnp.ones((8, HD), jnp.float32)
    summed = lax.dot_general(
        ones,
        total,
        (((1,), (1,)), ((), ())),
        precision=lax.Precision.HIGHEST,
        preferred_element_type=jnp.float32,
    )
    squares[...] = summed[0:1, :]


def tail(gated, carry, rates, gain, direct, gate, pitch):
    rows, width = gate.shape
    poles = rates.shape[0] // pitch
    f32 = jnp.float32
    return call(
        functools.partial(tail_kernel, width // HD, pitch),
        (
            jax.ShapeDtypeStruct((width // HD, rows, HD), f32),
            jax.ShapeDtypeStruct((1, rows), f32),
        ),
        3000 * poles * rows * width,
        10 * rows * width,
        in_specs=[HBM] + [VMEM] * 4 + [HBM],
        scratch_shapes=[
            pltpu.VMEM((rows * pitch, HD), f32),
            pltpu.VMEM((rows * pitch, HD), f32),
            pltpu.VMEM((rows, width), gate.dtype),
            pltpu.SemaphoreType.DMA((4 if rows % 32 == 0 else 1,)),
            pltpu.SemaphoreType.DMA,
        ],
    )(far(gated), carry, rates, gain, direct, far(gate))


def places(runs):
    index = lax.axis_index("seq")
    return index // PLANE % runs, index % PLANE


def norm_kernel(channels, conv, squares, *outs):
    runs, rows, _ = outs[0].shape
    run, place = places(runs)
    scale = lax.rsqrt(squares[...] / channels + 1e-06)
    scale = jnp.transpose(jnp.broadcast_to(scale, (HD, rows)))
    for j in range(PLANE):
        for k in range(runs):
            outs[j][k] = (conv[(run ^ k) * PLANE + (place ^ j)] * scale).astype(outs[j].dtype)


def normalize(conv, squares, channels):
    heads, rows, _ = conv.shape
    message = jax.ShapeDtypeStruct((heads // PLANE, rows, HD), jnp.bfloat16)
    return call(
        functools.partial(norm_kernel, channels),
        (message,) * PLANE,
        heads * rows * HD,
        6 * heads * rows * HD,
    )(conv, squares)


def prefix_state(summary, rates, block_rows, axis):
    size = lax.axis_size(axis)
    place = lax.axis_index(axis)
    span = rates * jnp.float32(block_rows)

    def fade(blocks):
        return jnp.exp(-span * jnp.maximum(blocks, 0).astype(jnp.float32))

    strides = [1]
    while strides[-1] * 4 < size:
        strides.append(strides[-1] * 4)
    before, above = None, size
    for stride in reversed(strides):
        many = above // stride
        digit, inside = place // stride % many, place % above
        total = None if before is None else fade(digit * stride) * before
        for k in range(1, many):
            other = digit ^ k
            gap = other * stride - inside - 1
            sent = summary
            if before is not None:
                sent = fade(other * stride) * before + jnp.where(
                    digit < other, fade(gap) * summary, 0.0
                )
            got = lax.ppermute(sent, axis, [(i, i ^ (stride * k)) for i in range(size)])
            if before is None:
                gap = digit * stride - (inside - digit * stride + other * stride) - 1
                got = jnp.where(other < digit, fade(gap) * got, 0.0)
            total = got if total is None else total + got
        before, above = total, stride
    return before


def attend_kernel(block, pair, *refs):
    *parts, out, scores, values = refs
    _, runs, twice, _ = pair.shape
    rows = twice // 2
    per_block = block // rows
    turns = runs * PLANE // per_block
    own_run, own_place = places(runs)
    factor = LOG2E * HD ** (-0.5)
    row = lax.broadcasted_iota(jnp.int32, (block, block), 0)
    col = lax.broadcasted_iota(jnp.int32, (block, block), 1)
    visible = col <= row
    for k, part in enumerate(parts):
        for j in range(PLANE):
            values[own_run ^ k, own_place ^ j] = part[j]

    def piece(turn, first):
        run, inside = divmod(turn * per_block, PLANE)
        got = [pair[inside + i, run, first : first + rows, :] for i in range(per_block)]
        return jnp.concatenate(got, axis=0)

    def score(turn, part, top):
        got = lax.dot_general(
            piece(turn, 0),
            piece(part, rows),
            (((1,), (1,)), ((), ())),
            preferred_element_type=jnp.float32,
        )
        if part == turn:
            got = jnp.where(visible, got, -1e30)
        scores[turn % 2, :, part * block : (part + 1) * block] = got
        for lane in range(0, block, HD):
            one = got[:, lane : lane + HD]
            top = one if top is None else jnp.maximum(top, one)
        return top

    def weigh(turn, part, top, total, mixed):
        got = scores[turn % 2, :, part * block : (part + 1) * block]
        expo = jnp.exp2(got * factor - top)
        for lane in range(0, block, HD):
            total = total + expo[:, lane : lane + HD]
        run, inside = divmod(part * per_block, PLANE)
        value = values[run, inside : inside + per_block].reshape(block, HD)
        mixed = mixed + jnp.dot(
            expo.astype(jnp.bfloat16), value, preferred_element_type=jnp.float32
        )
        return total, mixed

    zero = jnp.zeros((block, HD), jnp.float32)
    top = score(0, 0, None)
    for turn in range(turns):
        peak = jnp.max(top, axis=1, keepdims=True) * factor
        top, total, mixed = None, zero, zero
        for part in range(turn + 2):
            if turn + 1 < turns:
                top = score(turn + 1, part, top)
            if part <= turn:
                total, mixed = weigh(turn, part, peak, total, mixed)
        mixed = mixed / jnp.sum(total, axis=1, keepdims=True)
        out[turn * per_block : (turn + 1) * per_block] = mixed.astype(out.dtype).reshape(
            per_block, rows, HD
        )


def attend(pair, parts):
    _, runs, twice, _ = pair.shape
    rows = twice // 2
    block = rows
    while block < 256 and PLANE * rows % (2 * block) == 0:
        block *= 2
    length = runs * PLANE * rows
    return call(
        functools.partial(attend_kernel, block),
        jax.ShapeDtypeStruct((runs * PLANE, rows, HD), jnp.bfloat16),
        2 * length * length * HD,
        8 * length * HD,
        length * length // 2,
        scratch_shapes=[
            pltpu.VMEM((2, block, length), jnp.float32),
            pltpu.VMEM((runs, PLANE, rows, HD), jnp.bfloat16),
        ],
    )(pair, *parts)


def gathered_head(query, key, value, first_row):
    count, step = key.shape[0], math.gcd(key.shape[0], 1024)
    query_pos = first_row + jnp.arange(query.shape[0], dtype=jnp.int32)

    def one(turn, carried):
        top, total, mixed = carried
        keys = lax.dynamic_slice_in_dim(key, turn * step, step, 0)
        values = lax.dynamic_slice_in_dim(value, turn * step, step, 0)
        scores = jnp.dot(query, keys.T, preferred_element_type=jnp.float32) * HD ** (-0.5)
        visible = (turn * step + jnp.arange(step, dtype=jnp.int32))[None, :] <= query_pos[:, None]
        scores = jnp.where(visible, scores, -1e30)
        new_top = jnp.maximum(top, jnp.max(scores, axis=1, keepdims=True))
        rescale = jnp.exp(top - new_top)
        expo = jnp.where(visible, jnp.exp(scores - new_top), 0.0)
        total = total * rescale + jnp.sum(expo, axis=1, keepdims=True)
        part = jnp.dot(expo.astype(jnp.bfloat16), values, preferred_element_type=jnp.float32)
        return new_top, total, mixed * rescale + part

    rows = query.shape[0]
    start = (
        jnp.full((rows, 1), -1e30, jnp.float32),
        jnp.zeros((rows, 1), jnp.float32),
        jnp.zeros((rows, HD), jnp.float32),
    )
    _, total, mixed = lax.fori_loop(0, count // step, one, start)
    return (mixed / total).astype(jnp.bfloat16)


def local(
    gate_outer, gate_inner, value_in, pole_rates, pole_weights, skip_gain, query_rows, key_rows
):
    rows, width = gate_outer.shape
    heads = width // HD
    size = lax.axis_size("seq")
    channels = width * lax.axis_size("chan")
    group_count = size // heads
    runs = heads // PLANE
    pitch = -(-heads // 8) * 8

    def exchange(array, members, stride=1):
        if members == 1:
            return array
        span = members * stride
        teams = [
            list(range(first + offset, first + span, stride))
            for first in range(0, size, span)
            for offset in range(stride)
        ]
        return lax.all_to_all(
            array, "seq", 0, 0, axis_index_groups=teams if members < size else None
        )

    def swap(array, distance):
        if distance == 0:
            return array
        return lax.ppermute(array, "seq", [(i, i ^ distance) for i in range(size)])

    gated, summary, rates, gain, direct, chunks = first(
        gate_inner, value_in, pole_rates, pole_weights, skip_gain[None, :], query_rows, key_rows, pitch
    )
    pair = exchange(chunks.reshape(runs, PLANE, 2 * rows, HD), runs, PLANE)
    carry = prefix_state(summary, rates, rows, "seq")
    conv, squares = tail(gated, carry, rates, gain, direct, gate_outer, pitch)
    messages = normalize(conv, lax.psum(squares, "chan"), channels)
    near = [swap(message, j) for j, message in enumerate(messages)]
    values = [swap(jnp.stack([part[k] for part in near]), k * PLANE) for k in range(runs)]
    pair = exchange(jnp.swapaxes(pair, 0, 1), PLANE)
    if group_count == 1:
        mixed = attend(pair, values)
    else:
        mine = lax.axis_index("seq") // heads
        others = [list(range(h, size, heads)) for h in range(heads)]
        gather = functools.partial(
            lax.all_gather, axis_name="seq", axis_index_groups=others, tiled=True
        )
        span = heads * rows
        run, place = places(runs)
        values = [
            jnp.stack(values)[run ^ (h // PLANE), place ^ (h % PLANE)] for h in range(heads)
        ]
        pair = jnp.swapaxes(pair, 0, 1)
        mixed = gathered_head(
            pair[:, :, :rows].reshape(span, HD),
            gather(pair[:, :, rows:].reshape(span, HD)),
            gather(jnp.concatenate(values)),
            mine * span,
        ).reshape(heads, rows, HD)
    return join_heads(exchange(mixed, heads))


def solution(mesh):
    rows = P("seq", "chan")
    poles = P(None, "chan")
    return jax.shard_map(
        local,
        mesh=mesh,
        in_specs=(rows, rows, rows, poles, poles, P("chan"), rows, rows),
        out_specs=rows,
        check_vma=False,
    )
```

time: 82.9 us -> 80 us (0.965)
  starting transfers between devices: 22 us -> 26.2 us
  Pallas kernels: 14.3 us -> 11.3 us
  waiting for transfers between devices: 22.6 us -> 20.3 us
  local copies, waits for them, and re-layouts: 2.4 us -> 1.12 us
    all_to_all x2, waiting for transfers between devices: 16 us -> 5.73 us  [exchange(): lax.all_to_all(array, 'seq', 0, 0, axis_index_groups=teams if members < s...]
    ppermute x0 -> x6, waiting for transfers between devices: none -> 9.84 us  [swap(): return lax.ppermute(array, 'seq', [(i, i ^ distance) for i in range(size)])]
    ppermute x0 -> x6, starting transfers between devices: none -> 8.12 us  [swap(): return lax.ppermute(array, 'seq', [(i, i ^ distance) for i in range(size)])]
    all_to_all x2, starting transfers between devices: 12.9 us -> 8.81 us  [exchange(): lax.all_to_all(array, 'seq', 0, 0, axis_index_groups=teams if members < s...]
    pallas_call x5 -> x4, Pallas kernels: 13.3 us -> 10.4 us  [the longest x1 4.12 us: attend(): call(functools.partial(attend_kernel, block), jax.ShapeDtypeStruct((runs...]
    unnamed x8 -> x0, local copies, waits for them, and re-layouts: 2.22 us -> none
    ppermute x6, waiting for transfers between devices: 6.52 us -> 4.71 us  [prefix_state(): got = lax.ppermute(sent, axis, [(i, i ^ stride * k) for i in range(size)])]
    all_to_all x0 -> x1, local copies, waits for them, and re-layouts: none -> 1.08 us  [exchange(): lax.all_to_all(array, 'seq', 0, 0, axis_index_groups=teams if members < s...]
  transfers between devices with their start and end apart: 8 -> 14, of which waited for: 3 -> 9; matrix products, arithmetic and copies ran while one was open for 1% -> 2% of each run, Pallas kernels for 7% -> 4%
where the time goes in v3:
time: 80 us; the launch traced here: 79.7 us
  starting transfers between devices  26.2 us (33%)
  blocking collectives  20.5 us (26%)
  waiting for transfers between devices  20.3 us (25%)
  Pallas kernels  11.3 us (14%)
  local copies, waits for them, and re-layouts  1.12 us (1%)
    all_to_all x1, blocking collectives, exchange(): lax.all_to_all(array, 'seq', 0, 0, axis_index_groups=teams if members < s...  18 us
    ppermute x6, waiting for transfers between devices, swap(): return lax.ppermute(array, 'seq', [(i, i ^ distance) for i in range(size)])  9.84 us
    ppermute x6, starting transfers between devices, prefix_state(): got = lax.ppermute(sent, axis, [(i, i ^ stride * k) for i in range(size)])  9.23 us
    all_to_all x2, starting transfers between devices, exchange(): lax.all_to_all(array, 'seq', 0, 0, axis_index_groups=teams if members < s...  8.81 us
    ppermute x6, starting transfers between devices, swap(): return lax.ppermute(array, 'seq', [(i, i ^ distance) for i in range(size)])  8.12 us
    all_to_all x2, waiting for transfers between devices, exchange(): lax.all_to_all(array, 'seq', 0, 0, axis_index_groups=teams if members < s...  5.73 us
    ppermute x6, waiting for transfers between devices, prefix_state(): got = lax.ppermute(sent, axis, [(i, i ^ stride * k) for i in range(size)])  4.71 us
    pallas_call x1, Pallas kernels, attend(): call(functools.partial(attend_kernel, block), jax.ShapeDtypeStruct((runs...  4.12 us
  transfers between devices with their start and end apart: 14, of which 9 were waited for; matrix products, arithmetic and copies ran while one was open for 2% of the time, Pallas kernels for 4%

profile of v3, /device:TPU:0, one launch (start us, length us, event | category | flops | bytes accessed | tf_op | source)
XLA Modules:
  0.0 79.7 jit_solution(16441819224306788840)
XLA Ops:
  0.0 3.3 %shard_map.82 = (f32[2048,128]{1,0:T(8,128)}, f32[128,128]{1,0:T(8,128)S(1)}, f32[128,128]{1,0:T(8,128)S(1)}, f32[128,128]{1,0:T(8,128)S(1)}, f32[16,128]{1,0:T(8,128)S(1)}, /*index=5*/bf16[16,256,128]{2,1,0:T(8,128)(2,1)}) custom-call(bf16[128,2048]{1,0:T(8,128)(2,1)} %refs_0_.1, bf16[128,2048]{1,0:T(8,128)(2,1)} %refs_1_.1, f32[8,2048]{1,0:T(8,128)} %refs_2_.1, ...), custom_call_target="tpu_custom_call" | custom-call | flops 4194304 | bytes 4194304 | tf_op jit(solution)/shard_map/pallas_call | solution.py:152
  3.3 3.1 %collective-permute-start = (f32[128,128]{1,0:T(8,128)S(1)}, f32[128,128]{1,0:T(8,128)S(1)}, u32[]{:S(2)}, u32[]{:S(2)}) collective-permute-start(f32[128,128]{1,0:T(8,128)S(1)} %get-tuple-element.20), channel_id=1, source_target_pairs={{0,8},{2,10},{4,12},{6,14},{8,0},{10,2},{12,4},{14,6},{16,24},{18,... | collective-permute-start | bytes 196616 | tf_op jit(solution)/shard_map/ppermute | solution.py:307
  6.4 2.6 %collective-permute-start.1 = (f32[128,128]{1,0:T(8,128)S(1)}, f32[128,128]{1,0:T(8,128)S(1)}, u32[]{:S(2)}, u32[]{:S(2)}) collective-permute-start(f32[128,128]{1,0:T(8,128)S(1)} %get-tuple-element.20), channel_id=1, source_target_pairs={{0,16},{2,18},{4,20},{6,22},{8,24},{10,26},{12,28},{14,30},{16,0},... | collective-permute-start | bytes 196616 | tf_op jit(solution)/shard_map/ppermute | solution.py:307
  9.0 5.1 %all-to-all-start = ((bf16[4,4,256,128]{3,2,1,0:T(8,128)(2,1)}), bf16[4,4,256,128]{3,2,1,0:T(8,128)(2,1)S(1)}, u32[]{:S(2)}, u32[]{:S(2)}) async-start(bf16[4,4,256,128]{3,2,1,0:T(8,128)(2,1)} %bitcast.5), calls=%async_computation | async-start | bytes 2097152 | tf_op jit(solution)/shard_map/all_to_all | solution.py:447
  14.1 1.0 %collective-permute-done.2 = f32[128,128]{1,0:T(8,128)S(1)} collective-permute-done((f32[128,128]{1,0:T(8,128)S(1)}, f32[128,128]{1,0:T(8,128)S(1)}, u32[]{:S(2)}, u32[]{:S(2)}) %collective-permute-start.2) | collective-permute-done | bytes 65568 | tf_op jit(solution)/shard_map/ppermute | solution.py:307
  15.0 0.1 select_add_fusion.2
  15.1 0.1 select_add_fusion.1
  15.2 1.6 %collective-permute-start.4 = (f32[128,128]{1,0:T(8,128)S(1)}, f32[128,128]{1,0:T(8,128)S(1)}, u32[]{:S(2)}, u32[]{:S(2)}) collective-permute-start(f32[128,128]{1,0:T(8,128)S(1)} %get-tuple-element.31), channel_id=1, source_target_pairs={{0,4},{2,6},{4,0},{6,2},{8,12},{10,14},{12,8},{14,10},{16,20},{18,... | collective-permute-start | bytes 196616 | tf_op jit(solution)/shard_map/ppermute | solution.py:307
  16.8 1.4 %collective-permute-start.5 = (f32[128,128]{1,0:T(8,128)S(1)}, f32[128,128]{1,0:T(8,128)S(1)}, u32[]{:S(2)}, u32[]{:S(2)}) collective-permute-start(f32[128,128]{1,0:T(8,128)S(1)} %get-tuple-element.32), channel_id=1, source_target_pairs={{0,6},{2,4},{4,2},{6,0},{8,14},{10,12},{12,10},{14,8},{16,22},{18,... | collective-permute-start | bytes 196616 | tf_op jit(solution)/shard_map/ppermute | solution.py:307
  18.2 0.5 collective-permute-start.3
  18.7 0.9 %collective-permute-done.4 = f32[128,128]{1,0:T(8,128)S(1)} collective-permute-done((f32[128,128]{1,0:T(8,128)S(1)}, f32[128,128]{1,0:T(8,128)S(1)}, u32[]{:S(2)}, u32[]{:S(2)}) %collective-permute-start.4) | collective-permute-done | bytes 65568 | tf_op jit(solution)/shard_map/ppermute | solution.py:307
  19.6 2.3 %collective-permute-done.5 = f32[128,128]{1,0:T(8,128)S(1)} collective-permute-done((f32[128,128]{1,0:T(8,128)S(1)}, f32[128,128]{1,0:T(8,128)S(1)}, u32[]{:S(2)}, u32[]{:S(2)}) %collective-permute-start.5) | collective-permute-done | bytes 65568 | tf_op jit(solution)/shard_map/ppermute | solution.py:307
  21.9 0.5 collective-permute-done.3
  22.5 2.8 %shard_map.83 = (f32[16,128,128]{2,1,0:T(8,128)S(1)}, f32[1,128]{1,0:T(1,128)S(1)}) custom-call(f32[2048,128]{1,0:T(8,128)} %get-tuple-element.18.kept, f32[128,128]{1,0:T(8,128)S(1)} %add_add_fusion.carry, f32[128,128]{1,0:T(8,128)S(1)} %get-tuple-element.19.rates, f32[128,128]{1,0:T(8,128)S(1)} %get-tuple-element.21.gain, ...), custom_call_target="tpu_custom_call" | custom-call | flops 6291456000 | bytes 2621440 | tf_op jit(solution)/shard_map/pallas_call | solution.py:238
  25.4 2.5 %psum.7.squares = f32[1,128]{1,0:T(1,128)S(1)} all-reduce(f32[1,128]{1,0:T(1,128)S(1)} %get-tuple-element.24), channel_id=1, replica_groups=mesh['seq'=16,'chan'=2] {'chan'}, use_global_device_ids=true, to_apply=%region_0.1 | all-reduce | flops 128 | bytes 1024 | tf_op jit(solution)/shard_map/psum | solution.py:462
  27.8 0.1 shard_map.84
  28.0 1.0 %collective-permute-start.6 = (bf16[4,128,128]{2,1,0:T(8,128)(2,1)S(1)}, bf16[4,128,128]{2,1,0:T(8,128)(2,1)S(1)}, u32[]{:S(2)}, u32[]{:S(2)}) collective-permute-start(bf16[4,128,128]{2,1,0:T(8,128)(2,1)S(1)} %get-tuple-element.26), channel_id=1, source_target_pairs={{0,2},{2,0},{4,6},{6,4},{8,10},{10,8},{12,14},{14,12},{16,18},{18,... | collective-permute-start | bytes 393224 | tf_op jit(solution)/shard_map/ppermute | solution.py:454
  29.0 1.3 %collective-permute-start.7 = (bf16[4,128,128]{2,1,0:T(8,128)(2,1)S(1)}, bf16[4,128,128]{2,1,0:T(8,128)(2,1)S(1)}, u32[]{:S(2)}, u32[]{:S(2)}) collective-permute-start(bf16[4,128,128]{2,1,0:T(8,128)(2,1)S(1)} %get-tuple-element.27), channel_id=1, source_target_pairs={{0,4},{2,6},{4,0},{6,2},{8,12},{10,14},{12,8},{14,10},{16,20},{18,... | collective-permute-start | bytes 393224 | tf_op jit(solution)/shard_map/ppermute | solution.py:454
  30.3 1.3 %collective-permute-start.8 = (bf16[4,128,128]{2,1,0:T(8,128)(2,1)S(1)}, bf16[4,128,128]{2,1,0:T(8,128)(2,1)S(1)}, u32[]{:S(2)}, u32[]{:S(2)}) collective-permute-start(bf16[4,128,128]{2,1,0:T(8,128)(2,1)S(1)} %get-tuple-element.28), channel_id=1, source_target_pairs={{0,6},{2,4},{4,2},{6,0},{8,14},{10,12},{12,10},{14,8},{16,22},{18,... | collective-permute-start | bytes 393224 | tf_op jit(solution)/shard_map/ppermute | solution.py:454
  31.5 2.8 %collective-permute-done.6 = bf16[4,128,128]{2,1,0:T(8,128)(2,1)S(1)} collective-permute-done((bf16[4,128,128]{2,1,0:T(8,128)(2,1)S(1)}, bf16[4,128,128]{2,1,0:T(8,128)(2,1)S(1)}, u32[]{:S(2)}, u32[]{:S(2)}) %collective-permute-start.6) | collective-permute-done | bytes 131104 | tf_op jit(solution)/shard_map/ppermute | solution.py:454
  34.4 4.5 %all-to-all-done = bf16[4,4,256,128]{3,2,1,0:T(8,128)(2,1)S(1)} async-done(((bf16[4,4,256,128]{3,2,1,0:T(8,128)(2,1)}), bf16[4,4,256,128]{3,2,1,0:T(8,128)(2,1)S(1)}, u32[]{:S(2)}, u32[]{:S(2)}) %all-to-all-start) | async-done | bytes 1048608 | tf_op jit(solution)/shard_map/all_to_all | solution.py:447
  39.0 1.1 %copy.12 = bf16[4,4,256,128]{3,2,0,1:T(8,128)(2,1)} copy(bf16[4,4,256,128]{3,2,1,0:T(8,128)(2,1)S(1)} %all-to-all-done) | data formatting | bytes 2097152 | tf_op jit(solution)/shard_map/all_to_all | solution.py:447
  40.0 3.7 %all-to-all-start.1 = ((bf16[4,4,256,128]{3,2,1,0:T(8,128)(2,1)}), bf16[4,4,256,128]{3,2,1,0:T(8,128)(2,1)S(1)}, u32[]{:S(2)}, u32[]{:S(2)}) async-start(bf16[4,4,256,128]{3,2,1,0:T(8,128)(2,1)} %bitcast.4), calls=%async_computation.1 | async-start | bytes 2097152 | tf_op jit(solution)/shard_map/all_to_all | solution.py:447
  43.8 1.5 %collective-permute-start.11 = (bf16[4,128,128]{2,1,0:T(8,128)(2,1)S(1)}, bf16[4,128,128]{2,1,0:T(8,128)(2,1)S(1)}, u32[]{:S(2)}, u32[]{:S(2)}) collective-permute-start(bf16[4,128,128]{2,1,0:T(8,128)(2,1)S(1)} %pad_maximum_fusion.3), channel_id=1, source_target_pairs={{0,24},{2,26},{4,28},{6,30},{8,16},{10,18},{12,20},{14,22},{16,8},... | collective-permute-start | bytes 393224 | tf_op jit(solution)/shard_map/ppermute | solution.py:454
  45.4 0.1 collective-permute-start.10
  45.5 3.0 %collective-permute-start.9 = (bf16[4,128,128]{2,1,0:T(8,128)(2,1)S(1)}, bf16[4,128,128]{2,1,0:T(8,128)(2,1)S(1)}, u32[]{:S(2)}, u32[]{:S(2)}) collective-permute-start(bf16[4,128,128]{2,1,0:T(8,128)(2,1)S(1)} %pad_maximum_fusion.1), channel_id=1, source_target_pairs={{0,8},{2,10},{4,12},{6,14},{8,0},{10,2},{12,4},{14,6},{16,24},{18,... | collective-permute-start | bytes 393224 | tf_op jit(solution)/shard_map/ppermute | solution.py:454
  48.5 3.7 %collective-permute-done.11.refs_3_ = bf16[4,128,128]{2,1,0:T(8,128)(2,1)S(1)} collective-permute-done((bf16[4,128,128]{2,1,0:T(8,128)(2,1)S(1)}, bf16[4,128,128]{2,1,0:T(8,128)(2,1)S(1)}, u32[]{:S(2)}, u32[]{:S(2)}) %collective-permute-start.11) | collective-permute-done | bytes 131104 | tf_op jit(solution)/shard_map/ppermute | solution.py:454
  52.1 3.3 %collective-permute-done.10.refs_2_ = bf16[4,128,128]{2,1,0:T(8,128)(2,1)S(1)} collective-permute-done((bf16[4,128,128]{2,1,0:T(8,128)(2,1)S(1)}, bf16[4,128,128]{2,1,0:T(8,128)(2,1)S(1)}, u32[]{:S(2)}, u32[]{:S(2)}) %collective-permute-start.10) | collective-permute-done | bytes 131104 | tf_op jit(solution)/shard_map/ppermute | solution.py:454
  55.5 1.2 %all-to-all-done.1.pair = bf16[4,4,256,128]{3,2,1,0:T(8,128)(2,1)S(1)} async-done(((bf16[4,4,256,128]{3,2,1,0:T(8,128)(2,1)}), bf16[4,4,256,128]{3,2,1,0:T(8,128)(2,1)S(1)}, u32[]{:S(2)}, u32[]{:S(2)}) %all-to-all-start.1) | async-done | bytes 1048608 | tf_op jit(solution)/shard_map/all_to_all | solution.py:447
  56.6 4.1 %shard_map.85 = bf16[16,128,128]{2,1,0:T(8,128)(2,1)S(1)} custom-call(bf16[4,4,256,128]{3,2,1,0:T(8,128)(2,1)S(1)} %all-to-all-done.1.pair, bf16[4,128,128]{2,1,0:T(8,128)(2,1)S(1)} %pad_maximum_fusion.refs_0_, bf16[4,128,128]{2,1,0:T(8,128)(2,1)S(1)} %collective-permute-done.9.refs_1_, bf16[4,128,128]{2,1,0:T(8,128)(2,1)S(1)} %collective-permute-done.10.refs_2_, ...), custom_call_target="tpu_custom_call" | custom-call | flops 1073741824 | bytes 2097152 | tf_op jit(solution)/shard_map/pallas_call | solution.py:386
  60.8 18.0 %all_to_all.15.source = bf16[16,128,128]{2,1,0:T(8,128)(2,1)S(1)} all-to-all(bf16[16,128,128]{2,1,0:T(8,128)(2,1)S(1)} %shard_map.85), channel_id=1, replica_groups=mesh['seq'=16,'chan'=2] {'seq'}, dimensions={0} | all-to-all | bytes 1048576 | tf_op jit(solution)/shard_map/all_to_all | solution.py:447
  78.8 0.9 %shard_map.86 = bf16[128,2048]{1,0:T(8,128)(2,1)} custom-call(bf16[16,128,128]{2,1,0:T(8,128)(2,1)S(1)} %all_to_all.15.source), custom_call_target="tpu_custom_call" | custom-call | bytes 1048576 | tf_op jit(solution)/shard_map/pallas_call | solution.py:56
  (15 shorter events, 0.2 us)
Async XLA Ops:
  3.3 10.8 %collective-permute-start = (f32[128,128]{1,0:T(8,128)S(1)}, f32[128,128]{1,0:T(8,128)S(1)}, u32[]{:S(2)}, u32[]{:S(2)}) collective-permute-start(f32[128,128]{1,0:T(8,128)S(1)} %get-tuple-element.20), channel_id=1, source_target_pairs={{0,8},{2,10},{4,12},{6,14},{8,0},{10,2},{12,4},{14,6},{16,24},{18,... | collective-permute-start | bytes 196616 | tf_op jit(solution)/shard_map/ppermute | solution.py:307
  6.4 7.7 %collective-permute-start.1 = (f32[128,128]{1,0:T(8,128)S(1)}, f32[128,128]{1,0:T(8,128)S(1)}, u32[]{:S(2)}, u32[]{:S(2)}) collective-permute-start(f32[128,128]{1,0:T(8,128)S(1)} %get-tuple-element.20), channel_id=1, source_target_pairs={{0,16},{2,18},{4,20},{6,22},{8,24},{10,26},{12,28},{14,30},{16,0},... | collective-permute-start | bytes 196616 | tf_op jit(solution)/shard_map/ppermute | solution.py:307
  9.0 6.1 %collective-permute-start.2 = (f32[128,128]{1,0:T(8,128)S(1)}, f32[128,128]{1,0:T(8,128)S(1)}, u32[]{:S(2)}, u32[]{:S(2)}) collective-permute-start(f32[128,128]{1,0:T(8,128)S(1)} %get-tuple-element.20), channel_id=1, source_target_pairs={{0,24},{2,26},{4,28},{6,30},{8,16},{10,18},{12,20},{14,22},{16,8},... | collective-permute-start | bytes 196616 | tf_op jit(solution)/shard_map/ppermute | solution.py:307
  9.0 30.0 %all-to-all-start = ((bf16[4,4,256,128]{3,2,1,0:T(8,128)(2,1)}), bf16[4,4,256,128]{3,2,1,0:T(8,128)(2,1)S(1)}, u32[]{:S(2)}, u32[]{:S(2)}) async-start(bf16[4,4,256,128]{3,2,1,0:T(8,128)(2,1)} %bitcast.5), calls=%async_computation | async-start | bytes 2097152 | tf_op jit(solution)/shard_map/all_to_all | solution.py:447
  15.2 4.4 %collective-permute-start.4 = (f32[128,128]{1,0:T(8,128)S(1)}, f32[128,128]{1,0:T(8,128)S(1)}, u32[]{:S(2)}, u32[]{:S(2)}) collective-permute-start(f32[128,128]{1,0:T(8,128)S(1)} %get-tuple-element.31), channel_id=1, source_target_pairs={{0,4},{2,6},{4,0},{6,2},{8,12},{10,14},{12,8},{14,10},{16,20},{18,... | collective-permute-start | bytes 196616 | tf_op jit(solution)/shard_map/ppermute | solution.py:307
  16.8 5.2 %collective-permute-start.5 = (f32[128,128]{1,0:T(8,128)S(1)}, f32[128,128]{1,0:T(8,128)S(1)}, u32[]{:S(2)}, u32[]{:S(2)}) collective-permute-start(f32[128,128]{1,0:T(8,128)S(1)} %get-tuple-element.32), channel_id=1, source_target_pairs={{0,6},{2,4},{4,2},{6,0},{8,14},{10,12},{12,10},{14,8},{16,22},{18,... | collective-permute-start | bytes 196616 | tf_op jit(solution)/shard_map/ppermute | solution.py:307
  18.2 4.3 %collective-permute-start.3 = (f32[128,128]{1,0:T(8,128)S(1)}, f32[128,128]{1,0:T(8,128)S(1)}, u32[]{:S(2)}, u32[]{:S(2)}) collective-permute-start(f32[128,128]{1,0:T(8,128)S(1)} %get-tuple-element.29), channel_id=1, source_target_pairs={{0,2},{2,0},{4,6},{6,4},{8,10},{10,8},{12,14},{14,12},{16,18},{18,... | collective-permute-start | bytes 196616 | tf_op jit(solution)/shard_map/ppermute | solution.py:307
  28.0 6.4 %collective-permute-start.6 = (bf16[4,128,128]{2,1,0:T(8,128)(2,1)S(1)}, bf16[4,128,128]{2,1,0:T(8,128)(2,1)S(1)}, u32[]{:S(2)}, u32[]{:S(2)}) collective-permute-start(bf16[4,128,128]{2,1,0:T(8,128)(2,1)S(1)} %get-tuple-element.26), channel_id=1, source_target_pairs={{0,2},{2,0},{4,6},{6,4},{8,10},{10,8},{12,14},{14,12},{16,18},{18,... | collective-permute-start | bytes 393224 | tf_op jit(solution)/shard_map/ppermute | solution.py:454
  29.0 14.7 %collective-permute-start.7 = (bf16[4,128,128]{2,1,0:T(8,128)(2,1)S(1)}, bf16[4,128,128]{2,1,0:T(8,128)(2,1)S(1)}, u32[]{:S(2)}, u32[]{:S(2)}) collective-permute-start(bf16[4,128,128]{2,1,0:T(8,128)(2,1)S(1)} %get-tuple-element.27), channel_id=1, source_target_pairs={{0,4},{2,6},{4,0},{6,2},{8,12},{10,14},{12,8},{14,10},{16,20},{18,... | collective-permute-start | bytes 393224 | tf_op jit(solution)/shard_map/ppermute | solution.py:454
  30.3 13.5 %collective-permute-start.8 = (bf16[4,128,128]{2,1,0:T(8,128)(2,1)S(1)}, bf16[4,128,128]{2,1,0:T(8,128)(2,1)S(1)}, u32[]{:S(2)}, u32[]{:S(2)}) collective-permute-start(bf16[4,128,128]{2,1,0:T(8,128)(2,1)S(1)} %get-tuple-element.28), channel_id=1, source_target_pairs={{0,6},{2,4},{4,2},{6,0},{8,14},{10,12},{12,10},{14,8},{16,22},{18,... | collective-permute-start | bytes 393224 | tf_op jit(solution)/shard_map/ppermute | solution.py:454
  40.0 16.6 %all-to-all-start.1 = ((bf16[4,4,256,128]{3,2,1,0:T(8,128)(2,1)}), bf16[4,4,256,128]{3,2,1,0:T(8,128)(2,1)S(1)}, u32[]{:S(2)}, u32[]{:S(2)}) async-start(bf16[4,4,256,128]{3,2,1,0:T(8,128)(2,1)} %bitcast.4), calls=%async_computation.1 | async-start | bytes 2097152 | tf_op jit(solution)/shard_map/all_to_all | solution.py:447
  43.8 8.3 %collective-permute-start.11 = (bf16[4,128,128]{2,1,0:T(8,128)(2,1)S(1)}, bf16[4,128,128]{2,1,0:T(8,128)(2,1)S(1)}, u32[]{:S(2)}, u32[]{:S(2)}) collective-permute-start(bf16[4,128,128]{2,1,0:T(8,128)(2,1)S(1)} %pad_maximum_fusion.3), channel_id=1, source_target_pairs={{0,24},{2,26},{4,28},{6,30},{8,16},{10,18},{12,20},{14,22},{16,8},... | collective-permute-start | bytes 393224 | tf_op jit(solution)/shard_map/ppermute | solution.py:454
  45.4 10.1 %collective-permute-start.10 = (bf16[4,128,128]{2,1,0:T(8,128)(2,1)S(1)}, bf16[4,128,128]{2,1,0:T(8,128)(2,1)S(1)}, u32[]{:S(2)}, u32[]{:S(2)}) collective-permute-start(bf16[4,128,128]{2,1,0:T(8,128)(2,1)S(1)} %pad_maximum_fusion.2), channel_id=1, source_target_pairs={{0,16},{2,18},{4,20},{6,22},{8,24},{10,26},{12,28},{14,30},{16,0},... | collective-permute-start | bytes 393224 | tf_op jit(solution)/shard_map/ppermute | solution.py:454
  45.5 10.0 %collective-permute-start.9 = (bf16[4,128,128]{2,1,0:T(8,128)(2,1)S(1)}, bf16[4,128,128]{2,1,0:T(8,128)(2,1)S(1)}, u32[]{:S(2)}, u32[]{:S(2)}) collective-permute-start(bf16[4,128,128]{2,1,0:T(8,128)(2,1)S(1)} %pad_maximum_fusion.1), channel_id=1, source_target_pairs={{0,8},{2,10},{4,12},{6,14},{8,0},{10,2},{12,4},{14,6},{16,24},{18,... | collective-permute-start | bytes 393224 | tf_op jit(solution)/shard_map/ppermute | solution.py:454

commit v4 on v3

--- a/solution.py
+++ b/solution.py
@@ -448,6 +448,11 @@
             array, "seq", 0, 0, axis_index_groups=teams if members < size else None
         )
 
+    def across(array):
+        if channels != 2 * width:
+            return lax.psum(array, "chan")
+        return array + lax.ppermute(array, "chan", [(0, 1), (1, 0)])
+
     def swap(array, distance):
         if distance == 0:
             return array
@@ -459,7 +464,7 @@
     pair = exchange(chunks.reshape(runs, PLANE, 2 * rows, HD), runs, PLANE)
     carry = prefix_state(summary, rates, rows, "seq")
     conv, squares = tail(gated, carry, rates, gain, direct, gate_outer, pitch)
-    messages = normalize(conv, lax.psum(squares, "chan"), channels)
+    messages = normalize(conv, across(squares), channels)
     near = [swap(message, j) for j, message in enumerate(messages)]
     values = [swap(jnp.stack([part[k] for part in near]), k * PLANE) for k in range(runs)]
     pair = exchange(jnp.swapaxes(pair, 0, 1), PLANE)

time: 80 us -> 79.9 us (level)
  blocking collectives: 20.5 us -> 18 us
  waiting for transfers between devices: 20.3 us -> 22.7 us
    psum x1 -> x0, blocking collectives: 2.47 us -> none  [local(): messages = normalize(conv, lax.psum(squares, 'chan'), channels)]
    all_to_all x2, waiting for transfers between devices: 5.73 us -> 7.01 us  [exchange(): lax.all_to_all(array, 'seq', 0, 0, axis_index_groups=teams if members < s...]
    ppermute x0 -> x1, waiting for transfers between devices: none -> 1.11 us  [across(): return array + lax.ppermute(array, 'chan', [(0, 1), (1, 0)])]
  transfers between devices with their start and end apart: 14 -> 15, of which waited for: 9 -> 10; matrix products, arithmetic and copies ran while one was open for 2% -> 2% of each run, Pallas kernels for 4% -> 4%
where the time goes in v4:
time: 79.9 us; the launch traced here: 79.6 us
  starting transfers between devices  26.2 us (33%)
  waiting for transfers between devices  22.7 us (28%)
  blocking collectives  18 us (23%)
  Pallas kernels  11.2 us (14%)
  local copies, waits for them, and re-layouts  1.12 us (1%)
    all_to_all x1, blocking collectives, exchange(): lax.all_to_all(array, 'seq', 0, 0, axis_index_groups=teams if members < s...  18 us
    ppermute x6, waiting for transfers between devices, swap(): return lax.ppermute(array, 'seq', [(i, i ^ distance) for i in range(size)])  9.84 us
    ppermute x6, starting transfers between devices, prefix_state(): got = lax.ppermute(sent, axis, [(i, i ^ stride * k) for i in range(size)])  9.23 us
    all_to_all x2, starting transfers between devices, exchange(): lax.all_to_all(array, 'seq', 0, 0, axis_index_groups=teams if members < s...  8.81 us
    ppermute x6, starting transfers between devices, swap(): return lax.ppermute(array, 'seq', [(i, i ^ distance) for i in range(size)])  8.12 us
    all_to_all x2, waiting for transfers between devices, exchange(): lax.all_to_all(array, 'seq', 0, 0, axis_index_groups=teams if members < s...  7.01 us
    ppermute x6, waiting for transfers between devices, prefix_state(): got = lax.ppermute(sent, axis, [(i, i ^ stride * k) for i in range(size)])  4.71 us
    pallas_call x1, Pallas kernels, attend(): call(functools.partial(attend_kernel, block), jax.ShapeDtypeStruct((runs...  4.12 us
  transfers between devices with their start and end apart: 15, of which 10 were waited for; matrix products, arithmetic and copies ran while one was open for 2% of the time, Pallas kernels for 4%

profile of v4, /device:TPU:0, one launch (start us, length us, event | category | flops | bytes accessed | tf_op | source)
XLA Modules:
  0.0 79.6 jit_solution(13505534236822199838)
XLA Ops:
  0.0 3.2 %shard_map.82 = (f32[2048,128]{1,0:T(8,128)}, f32[128,128]{1,0:T(8,128)S(1)}, f32[128,128]{1,0:T(8,128)S(1)}, f32[128,128]{1,0:T(8,128)S(1)}, f32[16,128]{1,0:T(8,128)S(1)}, /*index=5*/bf16[16,256,128]{2,1,0:T(8,128)(2,1)}) custom-call(bf16[128,2048]{1,0:T(8,128)(2,1)} %refs_0_.1, bf16[128,2048]{1,0:T(8,128)(2,1)} %refs_1_.1, f32[8,2048]{1,0:T(8,128)} %refs_2_.1, ...), custom_call_target="tpu_custom_call" | custom-call | flops 4194304 | bytes 4194304 | tf_op jit(solution)/shard_map/pallas_call | solution.py:152
  3.2 3.1 %collective-permute-start = (f32[128,128]{1,0:T(8,128)S(1)}, f32[128,128]{1,0:T(8,128)S(1)}, u32[]{:S(2)}, u32[]{:S(2)}) collective-permute-start(f32[128,128]{1,0:T(8,128)S(1)} %get-tuple-element.20), channel_id=1, source_target_pairs={{0,8},{2,10},{4,12},{6,14},{8,0},{10,2},{12,4},{14,6},{16,24},{18,... | collective-permute-start | bytes 196616 | tf_op jit(solution)/shard_map/ppermute | solution.py:307
  6.3 2.6 %collective-permute-start.1 = (f32[128,128]{1,0:T(8,128)S(1)}, f32[128,128]{1,0:T(8,128)S(1)}, u32[]{:S(2)}, u32[]{:S(2)}) collective-permute-start(f32[128,128]{1,0:T(8,128)S(1)} %get-tuple-element.20), channel_id=1, source_target_pairs={{0,16},{2,18},{4,20},{6,22},{8,24},{10,26},{12,28},{14,30},{16,0},... | collective-permute-start | bytes 196616 | tf_op jit(solution)/shard_map/ppermute | solution.py:307
  8.9 5.1 %all-to-all-start = ((bf16[4,4,256,128]{3,2,1,0:T(8,128)(2,1)}), bf16[4,4,256,128]{3,2,1,0:T(8,128)(2,1)S(1)}, u32[]{:S(2)}, u32[]{:S(2)}) async-start(bf16[4,4,256,128]{3,2,1,0:T(8,128)(2,1)} %bitcast.5), calls=%async_computation | async-start | bytes 2097152 | tf_op jit(solution)/shard_map/all_to_all | solution.py:447
  14.0 1.0 %collective-permute-done.2 = f32[128,128]{1,0:T(8,128)S(1)} collective-permute-done((f32[128,128]{1,0:T(8,128)S(1)}, f32[128,128]{1,0:T(8,128)S(1)}, u32[]{:S(2)}, u32[]{:S(2)}) %collective-permute-start.2) | collective-permute-done | bytes 65568 | tf_op jit(solution)/shard_map/ppermute | solution.py:307
  15.0 0.1 select_add_fusion.2
  15.1 1.6 %collective-permute-start.4 = (f32[128,128]{1,0:T(8,128)S(1)}, f32[128,128]{1,0:T(8,128)S(1)}, u32[]{:S(2)}, u32[]{:S(2)}) collective-permute-start(f32[128,128]{1,0:T(8,128)S(1)} %get-tuple-element.31), channel_id=1, source_target_pairs={{0,4},{2,6},{4,0},{6,2},{8,12},{10,14},{12,8},{14,10},{16,20},{18,... | collective-permute-start | bytes 196616 | tf_op jit(solution)/shard_map/ppermute | solution.py:307
  16.7 1.4 %collective-permute-start.5 = (f32[128,128]{1,0:T(8,128)S(1)}, f32[128,128]{1,0:T(8,128)S(1)}, u32[]{:S(2)}, u32[]{:S(2)}) collective-permute-start(f32[128,128]{1,0:T(8,128)S(1)} %get-tuple-element.32), channel_id=1, source_target_pairs={{0,6},{2,4},{4,2},{6,0},{8,14},{10,12},{12,10},{14,8},{16,22},{18,... | collective-permute-start | bytes 196616 | tf_op jit(solution)/shard_map/ppermute | solution.py:307
  18.1 0.5 collective-permute-start.3
  18.7 0.9 %collective-permute-done.4 = f32[128,128]{1,0:T(8,128)S(1)} collective-permute-done((f32[128,128]{1,0:T(8,128)S(1)}, f32[128,128]{1,0:T(8,128)S(1)}, u32[]{:S(2)}, u32[]{:S(2)}) %collective-permute-start.4) | collective-permute-done | bytes 65568 | tf_op jit(solution)/shard_map/ppermute | solution.py:307
  19.5 2.3 %collective-permute-done.5 = f32[128,128]{1,0:T(8,128)S(1)} collective-permute-done((f32[128,128]{1,0:T(8,128)S(1)}, f32[128,128]{1,0:T(8,128)S(1)}, u32[]{:S(2)}, u32[]{:S(2)}) %collective-permute-start.5) | collective-permute-done | bytes 65568 | tf_op jit(solution)/shard_map/ppermute | solution.py:307
  21.9 0.5 collective-permute-done.3
  22.4 2.8 %shard_map.83 = (f32[16,128,128]{2,1,0:T(8,128)S(1)}, f32[1,128]{1,0:T(1,128)S(1)}) custom-call(f32[2048,128]{1,0:T(8,128)} %get-tuple-element.18.kept, f32[128,128]{1,0:T(8,128)S(1)} %add_add_fusion.carry, f32[128,128]{1,0:T(8,128)S(1)} %get-tuple-element.19.rates, f32[128,128]{1,0:T(8,128)S(1)} %get-tuple-element.21.gain, ...), custom_call_target="tpu_custom_call" | custom-call | flops 6291456000 | bytes 2621440 | tf_op jit(solution)/shard_map/pallas_call | solution.py:238
  25.3 0.1 collective-permute-start.6
  25.4 1.1 %collective-permute-done.6 = f32[1,128]{1,0:T(1,128)S(1)} collective-permute-done((f32[1,128]{1,0:T(1,128)S(1)}, f32[1,128]{1,0:T(1,128)S(1)}, u32[]{:S(2)}, u32[]{:S(2)}) %collective-permute-start.6) | collective-permute-done | bytes 544 | tf_op jit(solution)/shard_map/ppermute | solution.py:454
  26.5 0.1 shard_map.84
  26.6 1.0 %collective-permute-start.7 = (bf16[4,128,128]{2,1,0:T(8,128)(2,1)S(1)}, bf16[4,128,128]{2,1,0:T(8,128)(2,1)S(1)}, u32[]{:S(2)}, u32[]{:S(2)}) collective-permute-start(bf16[4,128,128]{2,1,0:T(8,128)(2,1)S(1)} %get-tuple-element.26), channel_id=1, source_target_pairs={{0,2},{2,0},{4,6},{6,4},{8,10},{10,8},{12,14},{14,12},{16,18},{18,... | collective-permute-start | bytes 393224 | tf_op jit(solution)/shard_map/ppermute | solution.py:459
  27.7 1.3 %collective-permute-start.8 = (bf16[4,128,128]{2,1,0:T(8,128)(2,1)S(1)}, bf16[4,128,128]{2,1,0:T(8,128)(2,1)S(1)}, u32[]{:S(2)}, u32[]{:S(2)}) collective-permute-start(bf16[4,128,128]{2,1,0:T(8,128)(2,1)S(1)} %get-tuple-element.27), channel_id=1, source_target_pairs={{0,4},{2,6},{4,0},{6,2},{8,12},{10,14},{12,8},{14,10},{16,20},{18,... | collective-permute-start | bytes 393224 | tf_op jit(solution)/shard_map/ppermute | solution.py:459
  28.9 1.3 %collective-permute-start.9 = (bf16[4,128,128]{2,1,0:T(8,128)(2,1)S(1)}, bf16[4,128,128]{2,1,0:T(8,128)(2,1)S(1)}, u32[]{:S(2)}, u32[]{:S(2)}) collective-permute-start(bf16[4,128,128]{2,1,0:T(8,128)(2,1)S(1)} %get-tuple-element.28), channel_id=1, source_target_pairs={{0,6},{2,4},{4,2},{6,0},{8,14},{10,12},{12,10},{14,8},{16,22},{18,... | collective-permute-start | bytes 393224 | tf_op jit(solution)/shard_map/ppermute | solution.py:459
  30.2 2.8 %collective-permute-done.7 = bf16[4,128,128]{2,1,0:T(8,128)(2,1)S(1)} collective-permute-done((bf16[4,128,128]{2,1,0:T(8,128)(2,1)S(1)}, bf16[4,128,128]{2,1,0:T(8,128)(2,1)S(1)}, u32[]{:S(2)}, u32[]{:S(2)}) %collective-permute-start.7) | collective-permute-done | bytes 131104 | tf_op jit(solution)/shard_map/ppermute | solution.py:459
  33.1 5.8 %all-to-all-done = bf16[4,4,256,128]{3,2,1,0:T(8,128)(2,1)S(1)} async-done(((bf16[4,4,256,128]{3,2,1,0:T(8,128)(2,1)}), bf16[4,4,256,128]{3,2,1,0:T(8,128)(2,1)S(1)}, u32[]{:S(2)}, u32[]{:S(2)}) %all-to-all-start) | async-done | bytes 1048608 | tf_op jit(solution)/shard_map/all_to_all | solution.py:447
  38.9 1.1 %copy.12 = bf16[4,4,256,128]{3,2,0,1:T(8,128)(2,1)} copy(bf16[4,4,256,128]{3,2,1,0:T(8,128)(2,1)S(1)} %all-to-all-done) | data formatting | bytes 2097152 | tf_op jit(solution)/shard_map/all_to_all | solution.py:447
  40.0 3.7 %all-to-all-start.1 = ((bf16[4,4,256,128]{3,2,1,0:T(8,128)(2,1)}), bf16[4,4,256,128]{3,2,1,0:T(8,128)(2,1)S(1)}, u32[]{:S(2)}, u32[]{:S(2)}) async-start(bf16[4,4,256,128]{3,2,1,0:T(8,128)(2,1)} %bitcast.4), calls=%async_computation.1 | async-start | bytes 2097152 | tf_op jit(solution)/shard_map/all_to_all | solution.py:447
  43.8 1.5 %collective-permute-start.12 = (bf16[4,128,128]{2,1,0:T(8,128)(2,1)S(1)}, bf16[4,128,128]{2,1,0:T(8,128)(2,1)S(1)}, u32[]{:S(2)}, u32[]{:S(2)}) collective-permute-start(bf16[4,128,128]{2,1,0:T(8,128)(2,1)S(1)} %pad_maximum_fusion.3), channel_id=1, source_target_pairs={{0,24},{2,26},{4,28},{6,30},{8,16},{10,18},{12,20},{14,22},{16,8},... | collective-permute-start | bytes 393224 | tf_op jit(solution)/shard_map/ppermute | solution.py:459
  45.3 0.1 collective-permute-start.11
  45.4 3.0 %collective-permute-start.10 = (bf16[4,128,128]{2,1,0:T(8,128)(2,1)S(1)}, bf16[4,128,128]{2,1,0:T(8,128)(2,1)S(1)}, u32[]{:S(2)}, u32[]{:S(2)}) collective-permute-start(bf16[4,128,128]{2,1,0:T(8,128)(2,1)S(1)} %pad_maximum_fusion.1), channel_id=1, source_target_pairs={{0,8},{2,10},{4,12},{6,14},{8,0},{10,2},{12,4},{14,6},{16,24},{18,... | collective-permute-start | bytes 393224 | tf_op jit(solution)/shard_map/ppermute | solution.py:459
  48.4 3.7 %collective-permute-done.12.refs_3_ = bf16[4,128,128]{2,1,0:T(8,128)(2,1)S(1)} collective-permute-done((bf16[4,128,128]{2,1,0:T(8,128)(2,1)S(1)}, bf16[4,128,128]{2,1,0:T(8,128)(2,1)S(1)}, u32[]{:S(2)}, u32[]{:S(2)}) %collective-permute-start.12) | collective-permute-done | bytes 131104 | tf_op jit(solution)/shard_map/ppermute | solution.py:459
  52.1 3.3 %collective-permute-done.11.refs_2_ = bf16[4,128,128]{2,1,0:T(8,128)(2,1)S(1)} collective-permute-done((bf16[4,128,128]{2,1,0:T(8,128)(2,1)S(1)}, bf16[4,128,128]{2,1,0:T(8,128)(2,1)S(1)}, u32[]{:S(2)}, u32[]{:S(2)}) %collective-permute-start.11) | collective-permute-done | bytes 131104 | tf_op jit(solution)/shard_map/ppermute | solution.py:459
  55.4 1.2 %all-to-all-done.1.pair = bf16[4,4,256,128]{3,2,1,0:T(8,128)(2,1)S(1)} async-done(((bf16[4,4,256,128]{3,2,1,0:T(8,128)(2,1)}), bf16[4,4,256,128]{3,2,1,0:T(8,128)(2,1)S(1)}, u32[]{:S(2)}, u32[]{:S(2)}) %all-to-all-start.1) | async-done | bytes 1048608 | tf_op jit(solution)/shard_map/all_to_all | solution.py:447
  56.6 4.1 %shard_map.85 = bf16[16,128,128]{2,1,0:T(8,128)(2,1)S(1)} custom-call(bf16[4,4,256,128]{3,2,1,0:T(8,128)(2,1)S(1)} %all-to-all-done.1.pair, bf16[4,128,128]{2,1,0:T(8,128)(2,1)S(1)} %pad_maximum_fusion.refs_0_, bf16[4,128,128]{2,1,0:T(8,128)(2,1)S(1)} %collective-permute-done.10.refs_1_, bf16[4,128,128]{2,1,0:T(8,128)(2,1)S(1)} %collective-permute-done.11.refs_2_, ...), custom_call_target="tpu_custom_call" | custom-call | flops 1073741824 | bytes 2097152 | tf_op jit(solution)/shard_map/pallas_call | solution.py:386
  60.7 18.0 %all_to_all.15.source = bf16[16,128,128]{2,1,0:T(8,128)(2,1)S(1)} all-to-all(bf16[16,128,128]{2,1,0:T(8,128)(2,1)S(1)} %shard_map.85), channel_id=1, replica_groups=mesh['seq'=16,'chan'=2] {'seq'}, dimensions={0} | all-to-all | bytes 1048576 | tf_op jit(solution)/shard_map/all_to_all | solution.py:447
  78.7 0.9 %shard_map.86 = bf16[128,2048]{1,0:T(8,128)(2,1)} custom-call(bf16[16,128,128]{2,1,0:T(8,128)(2,1)S(1)} %all_to_all.15.source), custom_call_target="tpu_custom_call" | custom-call | bytes 1048576 | tf_op jit(solution)/shard_map/pallas_call | solution.py:56
  (17 shorter events, 0.2 us)
Async XLA Ops:
  3.2 10.8 %collective-permute-start = (f32[128,128]{1,0:T(8,128)S(1)}, f32[128,128]{1,0:T(8,128)S(1)}, u32[]{:S(2)}, u32[]{:S(2)}) collective-permute-start(f32[128,128]{1,0:T(8,128)S(1)} %get-tuple-element.20), channel_id=1, source_target_pairs={{0,8},{2,10},{4,12},{6,14},{8,0},{10,2},{12,4},{14,6},{16,24},{18,... | collective-permute-start | bytes 196616 | tf_op jit(solution)/shard_map/ppermute | solution.py:307
  6.3 7.7 %collective-permute-start.1 = (f32[128,128]{1,0:T(8,128)S(1)}, f32[128,128]{1,0:T(8,128)S(1)}, u32[]{:S(2)}, u32[]{:S(2)}) collective-permute-start(f32[128,128]{1,0:T(8,128)S(1)} %get-tuple-element.20), channel_id=1, source_target_pairs={{0,16},{2,18},{4,20},{6,22},{8,24},{10,26},{12,28},{14,30},{16,0},... | collective-permute-start | bytes 196616 | tf_op jit(solution)/shard_map/ppermute | solution.py:307
  8.9 6.1 %collective-permute-start.2 = (f32[128,128]{1,0:T(8,128)S(1)}, f32[128,128]{1,0:T(8,128)S(1)}, u32[]{:S(2)}, u32[]{:S(2)}) collective-permute-start(f32[128,128]{1,0:T(8,128)S(1)} %get-tuple-element.20), channel_id=1, source_target_pairs={{0,24},{2,26},{4,28},{6,30},{8,16},{10,18},{12,20},{14,22},{16,8},... | collective-permute-start | bytes 196616 | tf_op jit(solution)/shard_map/ppermute | solution.py:307
  8.9 30.0 %all-to-all-start = ((bf16[4,4,256,128]{3,2,1,0:T(8,128)(2,1)}), bf16[4,4,256,128]{3,2,1,0:T(8,128)(2,1)S(1)}, u32[]{:S(2)}, u32[]{:S(2)}) async-start(bf16[4,4,256,128]{3,2,1,0:T(8,128)(2,1)} %bitcast.5), calls=%async_computation | async-start | bytes 2097152 | tf_op jit(solution)/shard_map/all_to_all | solution.py:447
  15.1 4.4 %collective-permute-start.4 = (f32[128,128]{1,0:T(8,128)S(1)}, f32[128,128]{1,0:T(8,128)S(1)}, u32[]{:S(2)}, u32[]{:S(2)}) collective-permute-start(f32[128,128]{1,0:T(8,128)S(1)} %get-tuple-element.31), channel_id=1, source_target_pairs={{0,4},{2,6},{4,0},{6,2},{8,12},{10,14},{12,8},{14,10},{16,20},{18,... | collective-permute-start | bytes 196616 | tf_op jit(solution)/shard_map/ppermute | solution.py:307
  16.7 5.2 %collective-permute-start.5 = (f32[128,128]{1,0:T(8,128)S(1)}, f32[128,128]{1,0:T(8,128)S(1)}, u32[]{:S(2)}, u32[]{:S(2)}) collective-permute-start(f32[128,128]{1,0:T(8,128)S(1)} %get-tuple-element.32), channel_id=1, source_target_pairs={{0,6},{2,4},{4,2},{6,0},{8,14},{10,12},{12,10},{14,8},{16,22},{18,... | collective-permute-start | bytes 196616 | tf_op jit(solution)/shard_map/ppermute | solution.py:307
  18.1 4.3 %collective-permute-start.3 = (f32[128,128]{1,0:T(8,128)S(1)}, f32[128,128]{1,0:T(8,128)S(1)}, u32[]{:S(2)}, u32[]{:S(2)}) collective-permute-start(f32[128,128]{1,0:T(8,128)S(1)} %get-tuple-element.29), channel_id=1, source_target_pairs={{0,2},{2,0},{4,6},{6,4},{8,10},{10,8},{12,14},{14,12},{16,18},{18,... | collective-permute-start | bytes 196616 | tf_op jit(solution)/shard_map/ppermute | solution.py:307
  25.3 1.2 %collective-permute-start.6 = (f32[1,128]{1,0:T(1,128)S(1)}, f32[1,128]{1,0:T(1,128)S(1)}, u32[]{:S(2)}, u32[]{:S(2)}) collective-permute-start(f32[1,128]{1,0:T(1,128)S(1)} %get-tuple-element.24), channel_id=1, source_target_pairs={{0,1},{1,0},{2,3},{3,2},{4,5},{5,4},{6,7},{7,6},{8,9},{9,8},{10,11... | collective-permute-start | bytes 1544 | tf_op jit(solution)/shard_map/ppermute | solution.py:454
  26.6 6.4 %collective-permute-start.7 = (bf16[4,128,128]{2,1,0:T(8,128)(2,1)S(1)}, bf16[4,128,128]{2,1,0:T(8,128)(2,1)S(1)}, u32[]{:S(2)}, u32[]{:S(2)}) collective-permute-start(bf16[4,128,128]{2,1,0:T(8,128)(2,1)S(1)} %get-tuple-element.26), channel_id=1, source_target_pairs={{0,2},{2,0},{4,6},{6,4},{8,10},{10,8},{12,14},{14,12},{16,18},{18,... | collective-permute-start | bytes 393224 | tf_op jit(solution)/shard_map/ppermute | solution.py:459
  27.7 16.0 %collective-permute-start.8 = (bf16[4,128,128]{2,1,0:T(8,128)(2,1)S(1)}, bf16[4,128,128]{2,1,0:T(8,128)(2,1)S(1)}, u32[]{:S(2)}, u32[]{:S(2)}) collective-permute-start(bf16[4,128,128]{2,1,0:T(8,128)(2,1)S(1)} %get-tuple-element.27), channel_id=1, source_target_pairs={{0,4},{2,6},{4,0},{6,2},{8,12},{10,14},{12,8},{14,10},{16,20},{18,... | collective-permute-start | bytes 393224 | tf_op jit(solution)/shard_map/ppermute | solution.py:459
  28.9 14.8 %collective-permute-start.9 = (bf16[4,128,128]{2,1,0:T(8,128)(2,1)S(1)}, bf16[4,128,128]{2,1,0:T(8,128)(2,1)S(1)}, u32[]{:S(2)}, u32[]{:S(2)}) collective-permute-start(bf16[4,128,128]{2,1,0:T(8,128)(2,1)S(1)} %get-tuple-element.28), channel_id=1, source_target_pairs={{0,6},{2,4},{4,2},{6,0},{8,14},{10,12},{12,10},{14,8},{16,22},{18,... | collective-permute-start | bytes 393224 | tf_op jit(solution)/shard_map/ppermute | solution.py:459
  40.0 16.6 %all-to-all-start.1 = ((bf16[4,4,256,128]{3,2,1,0:T(8,128)(2,1)}), bf16[4,4,256,128]{3,2,1,0:T(8,128)(2,1)S(1)}, u32[]{:S(2)}, u32[]{:S(2)}) async-start(bf16[4,4,256,128]{3,2,1,0:T(8,128)(2,1)} %bitcast.4), calls=%async_computation.1 | async-start | bytes 2097152 | tf_op jit(solution)/shard_map/all_to_all | solution.py:447
  43.8 8.3 %collective-permute-start.12 = (bf16[4,128,128]{2,1,0:T(8,128)(2,1)S(1)}, bf16[4,128,128]{2,1,0:T(8,128)(2,1)S(1)}, u32[]{:S(2)}, u32[]{:S(2)}) collective-permute-start(bf16[4,128,128]{2,1,0:T(8,128)(2,1)S(1)} %pad_maximum_fusion.3), channel_id=1, source_target_pairs={{0,24},{2,26},{4,28},{6,30},{8,16},{10,18},{12,20},{14,22},{16,8},... | collective-permute-start | bytes 393224 | tf_op jit(solution)/shard_map/ppermute | solution.py:459
  45.3 10.1 %collective-permute-start.11 = (bf16[4,128,128]{2,1,0:T(8,128)(2,1)S(1)}, bf16[4,128,128]{2,1,0:T(8,128)(2,1)S(1)}, u32[]{:S(2)}, u32[]{:S(2)}) collective-permute-start(bf16[4,128,128]{2,1,0:T(8,128)(2,1)S(1)} %pad_maximum_fusion.2), channel_id=1, source_target_pairs={{0,16},{2,18},{4,20},{6,22},{8,24},{10,26},{12,28},{14,30},{16,0},... | collective-permute-start | bytes 393224 | tf_op jit(solution)/shard_map/ppermute | solution.py:459
  45.4 10.0 %collective-permute-start.10 = (bf16[4,128,128]{2,1,0:T(8,128)(2,1)S(1)}, bf16[4,128,128]{2,1,0:T(8,128)(2,1)S(1)}, u32[]{:S(2)}, u32[]{:S(2)}) collective-permute-start(bf16[4,128,128]{2,1,0:T(8,128)(2,1)S(1)} %pad_maximum_fusion.1), channel_id=1, source_target_pairs={{0,8},{2,10},{4,12},{6,14},{8,0},{10,2},{12,4},{14,6},{16,24},{18,... | collective-permute-start | bytes 393224 | tf_op jit(solution)/shard_map/ppermute | solution.py:459

commit v5 on v3

--- a/solution.py
+++ b/solution.py
@@ -21,7 +21,7 @@
 
 def near(array):
     return pltpu.with_memory_space_constraint(array, pltpu.VMEM)
-VMEM_CAP = 12 * 1024 * 1024
+VMEM_CAP = 20 * 1024 * 1024
 
 
 def call(body, out_shape, flops, moved, exps=0, **kwargs):
@@ -380,7 +380,7 @@
     _, runs, twice, _ = pair.shape
     rows = twice // 2
     block = rows
-    while block < 256 and PLANE * rows % (2 * block) == 0:
+    while block < 512 and PLANE * rows % (2 * block) == 0:
         block *= 2
     length = runs * PLANE * rows
     return call(

time: 80 us -> 80.2 us (level)
  no operation moved by 1% of the time
where the time goes in v5:
time: 80.2 us; the launch traced here: 79.9 us
  starting transfers between devices  26.2 us (33%)
  blocking collectives  20.5 us (26%)
  waiting for transfers between devices  20.3 us (25%)
  Pallas kernels  11.5 us (14%)
  local copies, waits for them, and re-layouts  1.12 us (1%)
    all_to_all x1, blocking collectives, exchange(): lax.all_to_all(array, 'seq', 0, 0, axis_index_groups=teams if members < s...  18 us
    ppermute x6, waiting for transfers between devices, swap(): return lax.ppermute(array, 'seq', [(i, i ^ distance) for i in range(size)])  9.84 us
    ppermute x6, starting transfers between devices, prefix_state(): got = lax.ppermute(sent, axis, [(i, i ^ stride * k) for i in range(size)])  9.23 us
    all_to_all x2, starting transfers between devices, exchange(): lax.all_to_all(array, 'seq', 0, 0, axis_index_groups=teams if members < s...  8.81 us
    ppermute x6, starting transfers between devices, swap(): return lax.ppermute(array, 'seq', [(i, i ^ distance) for i in range(size)])  8.12 us
    all_to_all x2, waiting for transfers between devices, exchange(): lax.all_to_all(array, 'seq', 0, 0, axis_index_groups=teams if members < s...  5.73 us
    ppermute x6, waiting for transfers between devices, prefix_state(): got = lax.ppermute(sent, axis, [(i, i ^ stride * k) for i in range(size)])  4.71 us
    pallas_call x1, Pallas kernels, attend(): call(functools.partial(attend_kernel, block), jax.ShapeDtypeStruct((runs...  4.3 us
  transfers between devices with their start and end apart: 14, of which 9 were waited for; matrix products, arithmetic and copies ran while one was open for 2% of the time, Pallas kernels for 4%

profile of v5, /device:TPU:0, one launch (start us, length us, event | category | flops | bytes accessed | tf_op | source)
XLA Modules:
  0.0 79.9 jit_solution(13498023649018342101)
XLA Ops:
  0.0 3.3 %shard_map.82 = (f32[2048,128]{1,0:T(8,128)}, f32[128,128]{1,0:T(8,128)S(1)}, f32[128,128]{1,0:T(8,128)S(1)}, f32[128,128]{1,0:T(8,128)S(1)}, f32[16,128]{1,0:T(8,128)S(1)}, /*index=5*/bf16[16,256,128]{2,1,0:T(8,128)(2,1)}) custom-call(bf16[128,2048]{1,0:T(8,128)(2,1)} %refs_0_.1, bf16[128,2048]{1,0:T(8,128)(2,1)} %refs_1_.1, f32[8,2048]{1,0:T(8,128)} %refs_2_.1, ...), custom_call_target="tpu_custom_call" | custom-call | flops 4194304 | bytes 4194304 | tf_op jit(solution)/shard_map/pallas_call | solution.py:152
  3.3 3.1 %collective-permute-start = (f32[128,128]{1,0:T(8,128)S(1)}, f32[128,128]{1,0:T(8,128)S(1)}, u32[]{:S(2)}, u32[]{:S(2)}) collective-permute-start(f32[128,128]{1,0:T(8,128)S(1)} %get-tuple-element.20), channel_id=1, source_target_pairs={{0,8},{2,10},{4,12},{6,14},{8,0},{10,2},{12,4},{14,6},{16,24},{18,... | collective-permute-start | bytes 196616 | tf_op jit(solution)/shard_map/ppermute | solution.py:307
  6.4 2.6 %collective-permute-start.1 = (f32[128,128]{1,0:T(8,128)S(1)}, f32[128,128]{1,0:T(8,128)S(1)}, u32[]{:S(2)}, u32[]{:S(2)}) collective-permute-start(f32[128,128]{1,0:T(8,128)S(1)} %get-tuple-element.20), channel_id=1, source_target_pairs={{0,16},{2,18},{4,20},{6,22},{8,24},{10,26},{12,28},{14,30},{16,0},... | collective-permute-start | bytes 196616 | tf_op jit(solution)/shard_map/ppermute | solution.py:307
  9.0 5.1 %all-to-all-start = ((bf16[4,4,256,128]{3,2,1,0:T(8,128)(2,1)}), bf16[4,4,256,128]{3,2,1,0:T(8,128)(2,1)S(1)}, u32[]{:S(2)}, u32[]{:S(2)}) async-start(bf16[4,4,256,128]{3,2,1,0:T(8,128)(2,1)} %bitcast.5), calls=%async_computation | async-start | bytes 2097152 | tf_op jit(solution)/shard_map/all_to_all | solution.py:447
  14.1 1.0 %collective-permute-done.2 = f32[128,128]{1,0:T(8,128)S(1)} collective-permute-done((f32[128,128]{1,0:T(8,128)S(1)}, f32[128,128]{1,0:T(8,128)S(1)}, u32[]{:S(2)}, u32[]{:S(2)}) %collective-permute-start.2) | collective-permute-done | bytes 65568 | tf_op jit(solution)/shard_map/ppermute | solution.py:307
  15.0 0.1 select_add_fusion.2
  15.1 0.1 select_add_fusion.1
  15.2 1.6 %collective-permute-start.4 = (f32[128,128]{1,0:T(8,128)S(1)}, f32[128,128]{1,0:T(8,128)S(1)}, u32[]{:S(2)}, u32[]{:S(2)}) collective-permute-start(f32[128,128]{1,0:T(8,128)S(1)} %get-tuple-element.31), channel_id=1, source_target_pairs={{0,4},{2,6},{4,0},{6,2},{8,12},{10,14},{12,8},{14,10},{16,20},{18,... | collective-permute-start | bytes 196616 | tf_op jit(solution)/shard_map/ppermute | solution.py:307
  16.8 1.4 %collective-permute-start.5 = (f32[128,128]{1,0:T(8,128)S(1)}, f32[128,128]{1,0:T(8,128)S(1)}, u32[]{:S(2)}, u32[]{:S(2)}) collective-permute-start(f32[128,128]{1,0:T(8,128)S(1)} %get-tuple-element.32), channel_id=1, source_target_pairs={{0,6},{2,4},{4,2},{6,0},{8,14},{10,12},{12,10},{14,8},{16,22},{18,... | collective-permute-start | bytes 196616 | tf_op jit(solution)/shard_map/ppermute | solution.py:307
  18.2 0.5 collective-permute-start.3
  18.7 0.9 %collective-permute-done.4 = f32[128,128]{1,0:T(8,128)S(1)} collective-permute-done((f32[128,128]{1,0:T(8,128)S(1)}, f32[128,128]{1,0:T(8,128)S(1)}, u32[]{:S(2)}, u32[]{:S(2)}) %collective-permute-start.4) | collective-permute-done | bytes 65568 | tf_op jit(solution)/shard_map/ppermute | solution.py:307
  19.6 2.3 %collective-permute-done.5 = f32[128,128]{1,0:T(8,128)S(1)} collective-permute-done((f32[128,128]{1,0:T(8,128)S(1)}, f32[128,128]{1,0:T(8,128)S(1)}, u32[]{:S(2)}, u32[]{:S(2)}) %collective-permute-start.5) | collective-permute-done | bytes 65568 | tf_op jit(solution)/shard_map/ppermute | solution.py:307
  21.9 0.5 collective-permute-done.3
  22.5 2.8 %shard_map.83 = (f32[16,128,128]{2,1,0:T(8,128)S(1)}, f32[1,128]{1,0:T(1,128)S(1)}) custom-call(f32[2048,128]{1,0:T(8,128)} %get-tuple-element.18.kept, f32[128,128]{1,0:T(8,128)S(1)} %add_add_fusion.carry, f32[128,128]{1,0:T(8,128)S(1)} %get-tuple-element.19.rates, f32[128,128]{1,0:T(8,128)S(1)} %get-tuple-element.21.gain, ...), custom_call_target="tpu_custom_call" | custom-call | flops 6291456000 | bytes 2621440 | tf_op jit(solution)/shard_map/pallas_call | solution.py:238
  25.4 2.5 %psum.7.squares = f32[1,128]{1,0:T(1,128)S(1)} all-reduce(f32[1,128]{1,0:T(1,128)S(1)} %get-tuple-element.24), channel_id=1, replica_groups=mesh['seq'=16,'chan'=2] {'chan'}, use_global_device_ids=true, to_apply=%region_0.1 | all-reduce | flops 128 | bytes 1024 | tf_op jit(solution)/shard_map/psum | solution.py:462
  27.8 0.1 shard_map.84
  28.0 1.0 %collective-permute-start.6 = (bf16[4,128,128]{2,1,0:T(8,128)(2,1)S(1)}, bf16[4,128,128]{2,1,0:T(8,128)(2,1)S(1)}, u32[]{:S(2)}, u32[]{:S(2)}) collective-permute-start(bf16[4,128,128]{2,1,0:T(8,128)(2,1)S(1)} %get-tuple-element.26), channel_id=1, source_target_pairs={{0,2},{2,0},{4,6},{6,4},{8,10},{10,8},{12,14},{14,12},{16,18},{18,... | collective-permute-start | bytes 393224 | tf_op jit(solution)/shard_map/ppermute | solution.py:454
  29.0 1.3 %collective-permute-start.7 = (bf16[4,128,128]{2,1,0:T(8,128)(2,1)S(1)}, bf16[4,128,128]{2,1,0:T(8,128)(2,1)S(1)}, u32[]{:S(2)}, u32[]{:S(2)}) collective-permute-start(bf16[4,128,128]{2,1,0:T(8,128)(2,1)S(1)} %get-tuple-element.27), channel_id=1, source_target_pairs={{0,4},{2,6},{4,0},{6,2},{8,12},{10,14},{12,8},{14,10},{16,20},{18,... | collective-permute-start | bytes 393224 | tf_op jit(solution)/shard_map/ppermute | solution.py:454
  30.3 1.3 %collective-permute-start.8 = (bf16[4,128,128]{2,1,0:T(8,128)(2,1)S(1)}, bf16[4,128,128]{2,1,0:T(8,128)(2,1)S(1)}, u32[]{:S(2)}, u32[]{:S(2)}) collective-permute-start(bf16[4,128,128]{2,1,0:T(8,128)(2,1)S(1)} %get-tuple-element.28), channel_id=1, source_target_pairs={{0,6},{2,4},{4,2},{6,0},{8,14},{10,12},{12,10},{14,8},{16,22},{18,... | collective-permute-start | bytes 393224 | tf_op jit(solution)/shard_map/ppermute | solution.py:454
  31.5 2.8 %collective-permute-done.6 = bf16[4,128,128]{2,1,0:T(8,128)(2,1)S(1)} collective-permute-done((bf16[4,128,128]{2,1,0:T(8,128)(2,1)S(1)}, bf16[4,128,128]{2,1,0:T(8,128)(2,1)S(1)}, u32[]{:S(2)}, u32[]{:S(2)}) %collective-permute-start.6) | collective-permute-done | bytes 131104 | tf_op jit(solution)/shard_map/ppermute | solution.py:454
  34.4 4.5 %all-to-all-done = bf16[4,4,256,128]{3,2,1,0:T(8,128)(2,1)S(1)} async-done(((bf16[4,4,256,128]{3,2,1,0:T(8,128)(2,1)}), bf16[4,4,256,128]{3,2,1,0:T(8,128)(2,1)S(1)}, u32[]{:S(2)}, u32[]{:S(2)}) %all-to-all-start) | async-done | bytes 1048608 | tf_op jit(solution)/shard_map/all_to_all | solution.py:447
  39.0 1.1 %copy.12 = bf16[4,4,256,128]{3,2,0,1:T(8,128)(2,1)} copy(bf16[4,4,256,128]{3,2,1,0:T(8,128)(2,1)S(1)} %all-to-all-done) | data formatting | bytes 2097152 | tf_op jit(solution)/shard_map/all_to_all | solution.py:447
  40.0 3.7 %all-to-all-start.1 = ((bf16[4,4,256,128]{3,2,1,0:T(8,128)(2,1)}), bf16[4,4,256,128]{3,2,1,0:T(8,128)(2,1)S(1)}, u32[]{:S(2)}, u32[]{:S(2)}) async-start(bf16[4,4,256,128]{3,2,1,0:T(8,128)(2,1)} %bitcast.4), calls=%async_computation.1 | async-start | bytes 2097152 | tf_op jit(solution)/shard_map/all_to_all | solution.py:447
  43.8 1.5 %collective-permute-start.11 = (bf16[4,128,128]{2,1,0:T(8,128)(2,1)S(1)}, bf16[4,128,128]{2,1,0:T(8,128)(2,1)S(1)}, u32[]{:S(2)}, u32[]{:S(2)}) collective-permute-start(bf16[4,128,128]{2,1,0:T(8,128)(2,1)S(1)} %pad_maximum_fusion.3), channel_id=1, source_target_pairs={{0,24},{2,26},{4,28},{6,30},{8,16},{10,18},{12,20},{14,22},{16,8},... | collective-permute-start | bytes 393224 | tf_op jit(solution)/shard_map/ppermute | solution.py:454
  45.4 0.1 collective-permute-start.10
  45.5 3.0 %collective-permute-start.9 = (bf16[4,128,128]{2,1,0:T(8,128)(2,1)S(1)}, bf16[4,128,128]{2,1,0:T(8,128)(2,1)S(1)}, u32[]{:S(2)}, u32[]{:S(2)}) collective-permute-start(bf16[4,128,128]{2,1,0:T(8,128)(2,1)S(1)} %pad_maximum_fusion.1), channel_id=1, source_target_pairs={{0,8},{2,10},{4,12},{6,14},{8,0},{10,2},{12,4},{14,6},{16,24},{18,... | collective-permute-start | bytes 393224 | tf_op jit(solution)/shard_map/ppermute | solution.py:454
  48.5 3.7 %collective-permute-done.11.refs_3_ = bf16[4,128,128]{2,1,0:T(8,128)(2,1)S(1)} collective-permute-done((bf16[4,128,128]{2,1,0:T(8,128)(2,1)S(1)}, bf16[4,128,128]{2,1,0:T(8,128)(2,1)S(1)}, u32[]{:S(2)}, u32[]{:S(2)}) %collective-permute-start.11) | collective-permute-done | bytes 131104 | tf_op jit(solution)/shard_map/ppermute | solution.py:454
  52.1 3.3 %collective-permute-done.10.refs_2_ = bf16[4,128,128]{2,1,0:T(8,128)(2,1)S(1)} collective-permute-done((bf16[4,128,128]{2,1,0:T(8,128)(2,1)S(1)}, bf16[4,128,128]{2,1,0:T(8,128)(2,1)S(1)}, u32[]{:S(2)}, u32[]{:S(2)}) %collective-permute-start.10) | collective-permute-done | bytes 131104 | tf_op jit(solution)/shard_map/ppermute | solution.py:454
  55.5 1.2 %all-to-all-done.1.pair = bf16[4,4,256,128]{3,2,1,0:T(8,128)(2,1)S(1)} async-done(((bf16[4,4,256,128]{3,2,1,0:T(8,128)(2,1)}), bf16[4,4,256,128]{3,2,1,0:T(8,128)(2,1)S(1)}, u32[]{:S(2)}, u32[]{:S(2)}) %all-to-all-start.1) | async-done | bytes 1048608 | tf_op jit(solution)/shard_map/all_to_all | solution.py:447
  56.6 4.3 %shard_map.85 = bf16[16,128,128]{2,1,0:T(8,128)(2,1)S(1)} custom-call(bf16[4,4,256,128]{3,2,1,0:T(8,128)(2,1)S(1)} %all-to-all-done.1.pair, bf16[4,128,128]{2,1,0:T(8,128)(2,1)S(1)} %pad_maximum_fusion.refs_0_, bf16[4,128,128]{2,1,0:T(8,128)(2,1)S(1)} %collective-permute-done.9.refs_1_, bf16[4,128,128]{2,1,0:T(8,128)(2,1)S(1)} %collective-permute-done.10.refs_2_, ...), custom_call_target="tpu_custom_call" | custom-call | flops 1073741824 | bytes 2097152 | tf_op jit(solution)/shard_map/pallas_call | solution.py:386
  60.9 18.0 %all_to_all.15.source = bf16[16,128,128]{2,1,0:T(8,128)(2,1)S(1)} all-to-all(bf16[16,128,128]{2,1,0:T(8,128)(2,1)S(1)} %shard_map.85), channel_id=1, replica_groups=mesh['seq'=16,'chan'=2] {'seq'}, dimensions={0} | all-to-all | bytes 1048576 | tf_op jit(solution)/shard_map/all_to_all | solution.py:447
  78.9 0.9 %shard_map.86 = bf16[128,2048]{1,0:T(8,128)(2,1)} custom-call(bf16[16,128,128]{2,1,0:T(8,128)(2,1)S(1)} %all_to_all.15.source), custom_call_target="tpu_custom_call" | custom-call | bytes 1048576 | tf_op jit(solution)/shard_map/pallas_call | solution.py:56
  (15 shorter events, 0.2 us)
Async XLA Ops:
  3.3 10.8 %collective-permute-start = (f32[128,128]{1,0:T(8,128)S(1)}, f32[128,128]{1,0:T(8,128)S(1)}, u32[]{:S(2)}, u32[]{:S(2)}) collective-permute-start(f32[128,128]{1,0:T(8,128)S(1)} %get-tuple-element.20), channel_id=1, source_target_pairs={{0,8},{2,10},{4,12},{6,14},{8,0},{10,2},{12,4},{14,6},{16,24},{18,... | collective-permute-start | bytes 196616 | tf_op jit(solution)/shard_map/ppermute | solution.py:307
  6.4 7.7 %collective-permute-start.1 = (f32[128,128]{1,0:T(8,128)S(1)}, f32[128,128]{1,0:T(8,128)S(1)}, u32[]{:S(2)}, u32[]{:S(2)}) collective-permute-start(f32[128,128]{1,0:T(8,128)S(1)} %get-tuple-element.20), channel_id=1, source_target_pairs={{0,16},{2,18},{4,20},{6,22},{8,24},{10,26},{12,28},{14,30},{16,0},... | collective-permute-start | bytes 196616 | tf_op jit(solution)/shard_map/ppermute | solution.py:307
  9.0 6.1 %collective-permute-start.2 = (f32[128,128]{1,0:T(8,128)S(1)}, f32[128,128]{1,0:T(8,128)S(1)}, u32[]{:S(2)}, u32[]{:S(2)}) collective-permute-start(f32[128,128]{1,0:T(8,128)S(1)} %get-tuple-element.20), channel_id=1, source_target_pairs={{0,24},{2,26},{4,28},{6,30},{8,16},{10,18},{12,20},{14,22},{16,8},... | collective-permute-start | bytes 196616 | tf_op jit(solution)/shard_map/ppermute | solution.py:307
  9.0 30.0 %all-to-all-start = ((bf16[4,4,256,128]{3,2,1,0:T(8,128)(2,1)}), bf16[4,4,256,128]{3,2,1,0:T(8,128)(2,1)S(1)}, u32[]{:S(2)}, u32[]{:S(2)}) async-start(bf16[4,4,256,128]{3,2,1,0:T(8,128)(2,1)} %bitcast.5), calls=%async_computation | async-start | bytes 2097152 | tf_op jit(solution)/shard_map/all_to_all | solution.py:447
  15.2 4.4 %collective-permute-start.4 = (f32[128,128]{1,0:T(8,128)S(1)}, f32[128,128]{1,0:T(8,128)S(1)}, u32[]{:S(2)}, u32[]{:S(2)}) collective-permute-start(f32[128,128]{1,0:T(8,128)S(1)} %get-tuple-element.31), channel_id=1, source_target_pairs={{0,4},{2,6},{4,0},{6,2},{8,12},{10,14},{12,8},{14,10},{16,20},{18,... | collective-permute-start | bytes 196616 | tf_op jit(solution)/shard_map/ppermute | solution.py:307
  16.8 5.2 %collective-permute-start.5 = (f32[128,128]{1,0:T(8,128)S(1)}, f32[128,128]{1,0:T(8,128)S(1)}, u32[]{:S(2)}, u32[]{:S(2)}) collective-permute-start(f32[128,128]{1,0:T(8,128)S(1)} %get-tuple-element.32), channel_id=1, source_target_pairs={{0,6},{2,4},{4,2},{6,0},{8,14},{10,12},{12,10},{14,8},{16,22},{18,... | collective-permute-start | bytes 196616 | tf_op jit(solution)/shard_map/ppermute | solution.py:307
  18.2 4.3 %collective-permute-start.3 = (f32[128,128]{1,0:T(8,128)S(1)}, f32[128,128]{1,0:T(8,128)S(1)}, u32[]{:S(2)}, u32[]{:S(2)}) collective-permute-start(f32[128,128]{1,0:T(8,128)S(1)} %get-tuple-element.29), channel_id=1, source_target_pairs={{0,2},{2,0},{4,6},{6,4},{8,10},{10,8},{12,14},{14,12},{16,18},{18,... | collective-permute-start | bytes 196616 | tf_op jit(solution)/shard_map/ppermute | solution.py:307
  28.0 6.4 %collective-permute-start.6 = (bf16[4,128,128]{2,1,0:T(8,128)(2,1)S(1)}, bf16[4,128,128]{2,1,0:T(8,128)(2,1)S(1)}, u32[]{:S(2)}, u32[]{:S(2)}) collective-permute-start(bf16[4,128,128]{2,1,0:T(8,128)(2,1)S(1)} %get-tuple-element.26), channel_id=1, source_target_pairs={{0,2},{2,0},{4,6},{6,4},{8,10},{10,8},{12,14},{14,12},{16,18},{18,... | collective-permute-start | bytes 393224 | tf_op jit(solution)/shard_map/ppermute | solution.py:454
  29.0 14.7 %collective-permute-start.7 = (bf16[4,128,128]{2,1,0:T(8,128)(2,1)S(1)}, bf16[4,128,128]{2,1,0:T(8,128)(2,1)S(1)}, u32[]{:S(2)}, u32[]{:S(2)}) collective-permute-start(bf16[4,128,128]{2,1,0:T(8,128)(2,1)S(1)} %get-tuple-element.27), channel_id=1, source_target_pairs={{0,4},{2,6},{4,0},{6,2},{8,12},{10,14},{12,8},{14,10},{16,20},{18,... | collective-permute-start | bytes 393224 | tf_op jit(solution)/shard_map/ppermute | solution.py:454
  30.3 13.5 %collective-permute-start.8 = (bf16[4,128,128]{2,1,0:T(8,128)(2,1)S(1)}, bf16[4,128,128]{2,1,0:T(8,128)(2,1)S(1)}, u32[]{:S(2)}, u32[]{:S(2)}) collective-permute-start(bf16[4,128,128]{2,1,0:T(8,128)(2,1)S(1)} %get-tuple-element.28), channel_id=1, source_target_pairs={{0,6},{2,4},{4,2},{6,0},{8,14},{10,12},{12,10},{14,8},{16,22},{18,... | collective-permute-start | bytes 393224 | tf_op jit(solution)/shard_map/ppermute | solution.py:454
  40.0 16.6 %all-to-all-start.1 = ((bf16[4,4,256,128]{3,2,1,0:T(8,128)(2,1)}), bf16[4,4,256,128]{3,2,1,0:T(8,128)(2,1)S(1)}, u32[]{:S(2)}, u32[]{:S(2)}) async-start(bf16[4,4,256,128]{3,2,1,0:T(8,128)(2,1)} %bitcast.4), calls=%async_computation.1 | async-start | bytes 2097152 | tf_op jit(solution)/shard_map/all_to_all | solution.py:447
  43.8 8.3 %collective-permute-start.11 = (bf16[4,128,128]{2,1,0:T(8,128)(2,1)S(1)}, bf16[4,128,128]{2,1,0:T(8,128)(2,1)S(1)}, u32[]{:S(2)}, u32[]{:S(2)}) collective-permute-start(bf16[4,128,128]{2,1,0:T(8,128)(2,1)S(1)} %pad_maximum_fusion.3), channel_id=1, source_target_pairs={{0,24},{2,26},{4,28},{6,30},{8,16},{10,18},{12,20},{14,22},{16,8},... | collective-permute-start | bytes 393224 | tf_op jit(solution)/shard_map/ppermute | solution.py:454
  45.4 10.1 %collective-permute-start.10 = (bf16[4,128,128]{2,1,0:T(8,128)(2,1)S(1)}, bf16[4,128,128]{2,1,0:T(8,128)(2,1)S(1)}, u32[]{:S(2)}, u32[]{:S(2)}) collective-permute-start(bf16[4,128,128]{2,1,0:T(8,128)(2,1)S(1)} %pad_maximum_fusion.2), channel_id=1, source_target_pairs={{0,16},{2,18},{4,20},{6,22},{8,24},{10,26},{12,28},{14,30},{16,0},... | collective-permute-start | bytes 393224 | tf_op jit(solution)/shard_map/ppermute | solution.py:454
  45.5 10.0 %collective-permute-start.9 = (bf16[4,128,128]{2,1,0:T(8,128)(2,1)S(1)}, bf16[4,128,128]{2,1,0:T(8,128)(2,1)S(1)}, u32[]{:S(2)}, u32[]{:S(2)}) collective-permute-start(bf16[4,128,128]{2,1,0:T(8,128)(2,1)S(1)} %pad_maximum_fusion.1), channel_id=1, source_target_pairs={{0,8},{2,10},{4,12},{6,14},{8,0},{10,2},{12,4},{14,6},{16,24},{18,... | collective-permute-start | bytes 393224 | tf_op jit(solution)/shard_map/ppermute | solution.py:454
